TPU v7x, 32 devices: a whole 2x2x4 slice. The times are simulated.
32 devices in a mesh: var: 16 (over z, y, core), win: 2 (over x).
Axes of the slice: x: 2, y: 2, z: 4, core: 2. Of those that a mesh axis runs over, the one named last changes fastest.
Arguments:
- series: float32 [64, 896, 96], P('var', 'win'), may hold values from -30 to 30
- target: float32 [64, 896, 96], P('var', 'win'), may hold values from -30 to 30
- valid_slots: int32 [896], P('win'), may hold values 0 or 1
- observed: int32 [64, 896, 96], P('var', 'win'), may hold values from 0 to 1
- embed_weight: float32 [96, 512], P(None, 'var'), may hold values from -0.625 to 0.625
- joint_proj: float32 [1, 512, 1536], P(None, 'var'), may hold values from -0.25 to 0.25
- out_proj: float32 [1, 512, 512], P(None, 'var'), may hold values from -1.5 to 1.5
- up_proj: float32 [1, 512, 2048], P(None, 'var'), may hold values from -0.25 to 0.25
- down_proj: float32 [1, 2048, 512], P(None, 'var'), may hold values from -0.125 to 0.125
- head_weight: float32 [512, 96], P('var'), may hold values from -0.25 to 0.25
- norm_params: float32 [1, 4, 512], P(None, None, 'var'), may hold values from -0.6 to 1.3
- embed_mean: float32 [96, 512], P(None, 'var'), may hold values from -0.001953125 to 0.001953125
- joint_mean: float32 [1, 512, 1536], P(None, 'var'), may hold values from -0.00048828125 to 0.00048828125
- out_mean: float32 [1, 512, 512], P(None, 'var'), may hold values from -0.00048828125 to 0.00048828125
- up_mean: float32 [1, 512, 2048], P(None, 'var'), may hold values from -0.00048828125 to 0.00048828125
- down_mean: float32 [1, 2048, 512], P(None, 'var'), may hold values from -0.00048828125 to 0.00048828125
- head_mean: float32 [512, 96], P('var'), may hold values from -0.001953125 to 0.001953125
- norm_mean: float32 [1, 4, 512], P(None, None, 'var'), may hold values from -0.00390625 to 0.00390625
- embed_square: float32 [96, 512], P(None, 'var'), may hold values from 4.045759e-09 to 6.417411e-08
- joint_square: float32 [1, 512, 1536], P(None, 'var'), may hold values from 2.5285993e-10 to 4.010882e-09
- out_square: float32 [1, 512, 512], P(None, 'var'), may hold values from 2.5285993e-10 to 4.010882e-09
- up_square: float32 [1, 512, 2048], P(None, 'var'), may hold values from 2.5285993e-10 to 4.010882e-09
- down_square: float32 [1, 2048, 512], P(None, 'var'), may hold values from 2.5285993e-10 to 4.010882e-09
- head_square: float32 [512, 96], P('var'), may hold values from 4.045759e-09 to 6.417411e-08
- norm_square: float32 [1, 4, 512], P(None, None, 'var'), may hold values from 1.6183035e-08 to 2.5634765e-07
Outputs:
- loss: float32 [1], replicated
- new_embed: float32 [96, 512], P(None, 'var')
- new_joint: float32 [1, 512, 1536], P(None, 'var')
- new_out: float32 [1, 512, 512], P(None, 'var')
- new_up: float32 [1, 512, 2048], P(None, 'var')
- new_down: float32 [1, 2048, 512], P(None, 'var')
- new_head: float32 [512, 96], P('var')
- norm_grad: float32 [1, 4, 512], P(None, None, 'var')
- next_embed_mean: float32 [96, 512], P(None, 'var')
- next_joint_mean: float32 [1, 512, 1536], P(None, 'var')
- next_out_mean: float32 [1, 512, 512], P(None, 'var')
- next_up_mean: float32 [1, 512, 2048], P(None, 'var')
- next_down_mean: float32 [1, 2048, 512], P(None, 'var')
- next_head_mean: float32 [512, 96], P('var')
- next_norm_mean: float32 [1, 4, 512], P(None, None, 'var')
- next_embed_square: float32 [96, 512], P(None, 'var')
- next_joint_square: float32 [1, 512, 1536], P(None, 'var')
- next_out_square: float32 [1, 512, 512], P(None, 'var')
- next_up_square: float32 [1, 512, 2048], P(None, 'var')
- next_down_square: float32 [1, 2048, 512], P(None, 'var')
- next_head_square: float32 [512, 96], P('var')
- next_norm_square: float32 [1, 4, 512], P(None, None, 'var')
All inputs are finite; a program needn't handle non-finite values. No bound on the sum of `valid_slots` on one device may be relied on, other than what follows from the above.
Results may differ from a plain program's by a relative error of at most 0.018.
Values may be sent and summed in bfloat16 or wider, within the bound.
No kernel may reach another device: no remote copies, remote signals or barrier semaphores. Data moves between devices by JAX's collectives and lax.ppermute only.
A program may use at most 320 MiB of HBM per device.

v0:
```python
from functools import partial

import jax
import jax.numpy as jnp
from jax import lax
from jax.sharding import PartitionSpec as P

HEADS = 8
HEAD_SIZE = 64
LAYERS = 1
STEP_NUMBER = 10


def passed_along(block, axis, distance):
    devices = range(lax.axis_size(axis))
    route = [((i - distance) % len(devices), i) for i in devices]
    return lax.ppermute(block, axis, route)


def layer_norm(resid, gain, shift):
    centre = jnp.mean(resid, -1, keepdims=True)
    offset = resid - centre
    spread = jnp.mean(offset * offset, -1, keepdims=True)
    return offset * lax.rsqrt(spread + 1e-05) * gain + shift


def adamw(weight, mean, square, grad, count_step):
    mean_next = 0.9 * mean + 0.1 * grad
    square_next = 0.999 * square + 0.001 * grad * grad
    mean_hat = mean_next / (1.0 - 0.9**count_step)
    square_hat = square_next / (1.0 - 0.999**count_step)
    weight_next = weight - 0.1 * (mean_hat / (jnp.sqrt(square_hat) + 1e-08) + 0.1 * weight)
    return (weight_next, mean_next, square_next)


def to_items(matrix, windows, local, parts):
    shaped = matrix.reshape(windows, local, parts, HEADS, HEAD_SIZE).transpose(0, 3, 1, 2, 4)
    return shaped.reshape(windows * HEADS, local, parts * HEAD_SIZE)


def from_items(items, windows, local, parts):
    shaped = items.reshape(windows, HEADS, local, parts, HEAD_SIZE).transpose(0, 2, 3, 1, 4)
    return shaped.reshape(windows * local, parts * HEADS * HEAD_SIZE)


def masked_scores(query_rows, key_portion, markers, query_pos, key_pos):
    score_matrix = (
        jnp.einsum("acn,azn->acz", query_rows, key_portion, preferred_element_type=jnp.float32)
        * 0.125
    )
    allowed = (markers[None, :] > 0.5) | (query_pos[:, None] == key_pos[None, :])
    return jnp.where(allowed[None], score_matrix, -1e30)


def absorb(state, query_rows, paired_keys, markers, query_pos, key_pos):
    peak, totals, accum = state
    score_matrix = masked_scores(
        query_rows, paired_keys[..., :HEAD_SIZE], markers, query_pos, key_pos
    )
    top_new = jnp.maximum(peak, jnp.max(score_matrix, -1))
    rescale = jnp.exp(peak - top_new)
    weights = jnp.exp(score_matrix - top_new[..., None])
    totals = totals * rescale + jnp.sum(weights, -1)
    reduced_weights = weights.astype(jnp.bfloat16)
    accum = accum * rescale[..., None] + jnp.einsum(
        "zsx,zxj->zsj",
        reduced_weights,
        paired_keys[..., HEAD_SIZE:],
        preferred_element_type=jnp.float32,
    )
    return (top_new, totals, accum)


def release(
    dquery, query_rows, paired_keys, markers, query_pos, key_pos, log_total, mixed_gradient, deltas
):
    key_portion = paired_keys[..., :HEAD_SIZE]
    value_rows = paired_keys[..., HEAD_SIZE:]
    score_matrix = masked_scores(query_rows, key_portion, markers, query_pos, key_pos)
    weights = jnp.exp(score_matrix - log_total[..., None])
    weight_gradient = jnp.einsum(
        "acn,azn->acz", mixed_gradient, value_rows, preferred_element_type=jnp.float32
    )
    score_gradient = (weights * (weight_gradient - deltas[..., None])).astype(jnp.bfloat16)
    reduced_weights = weights.astype(jnp.bfloat16)
    dquery = (
        dquery
        + jnp.einsum(
            "zsx,zxj->zsj", score_gradient, key_portion, preferred_element_type=jnp.float32
        )
        * 0.125
    )
    key_gradient = (
        jnp.einsum("fov,foc->fvc", score_gradient, query_rows, preferred_element_type=jnp.float32)
        * 0.125
    )
    value_gradient = jnp.einsum(
        "fov,foc->fvc", reduced_weights, mixed_gradient, preferred_element_type=jnp.float32
    )
    return (dquery, key_gradient, value_gradient)


def empty_state(blocks, length):
    return (
        jnp.full((blocks, length), -1e30, jnp.float32),
        jnp.zeros((blocks, length), jnp.float32),
        jnp.zeros((blocks, length, HEAD_SIZE), jnp.float32),
    )


def attend_forward(items, markers, position, group, local):
    blocks = items.shape[0]
    query_rows = items[..., :HEAD_SIZE]
    paired_keys = items[..., HEAD_SIZE:]
    query_pos = position * local + jnp.arange(local, dtype=jnp.int32)
    state = absorb(
        empty_state(blocks, local), query_rows, paired_keys, markers, query_pos, query_pos
    )

    def turn(counter, carry):
        moving, moving_marks, state = carry
        moving, moving_marks = passed_along((moving, moving_marks), "win", 1)
        key_pos = (position - counter) % group * local + jnp.arange(local, dtype=jnp.int32)
        return (
            moving,
            moving_marks,
            absorb(state, query_rows, moving, moving_marks, query_pos, key_pos),
        )

    _, _, state = lax.fori_loop(1, group, turn, (paired_keys, markers, state))
    peak, totals, accum = state
    mixed_full = accum / totals[..., None]
    return (mixed_full.astype(jnp.bfloat16), (mixed_full, peak + jnp.log(totals)))


def attend_backward(items, markers, mixed_gradient, kept, position, group, local):
    blocks = items.shape[0]
    mixed_full, log_total = kept
    query_rows = items[..., :HEAD_SIZE]
    deltas = jnp.sum(mixed_gradient.astype(jnp.float32) * mixed_full, -1)
    query_pos = position * local + jnp.arange(local, dtype=jnp.int32)

    def turn(counter, carry):
        moving, moving_marks, dquery, dpairs = carry
        key_pos = (position - counter) % group * local + jnp.arange(local, dtype=jnp.int32)
        dquery, key_gradient, value_gradient = release(
            dquery,
            query_rows,
            moving,
            moving_marks,
            query_pos,
            key_pos,
            log_total,
            mixed_gradient,
            deltas,
        )
        dpairs = passed_along(
            (dpairs + jnp.concatenate([key_gradient, value_gradient], -1)).astype(jnp.bfloat16),
            "win",
            1,
        ).astype(jnp.float32)
        moving, moving_marks = passed_along((moving, moving_marks), "win", 1)
        return (moving, moving_marks, dquery, dpairs)

    start = (
        items[..., HEAD_SIZE:],
        markers,
        jnp.zeros((blocks, local, HEAD_SIZE), jnp.float32),
        jnp.zeros((blocks, local, 2 * HEAD_SIZE), jnp.float32),
    )
    _, _, dquery, dpairs = lax.fori_loop(0, group, turn, start)
    return jnp.concatenate([dquery, dpairs], -1).astype(jnp.bfloat16)


def layer_forward(hidden, layer_weights, markers, position, group, windows, local):
    joint, out_mat, up_mat, down_mat, norms = layer_weights
    hidden_low = hidden.astype(jnp.bfloat16)
    items = to_items(
        jnp.dot(hidden_low, joint, preferred_element_type=jnp.float32).astype(jnp.bfloat16),
        windows,
        local,
        3,
    )
    mixed_items, kept_attn = attend_forward(items, markers, position, group, local)
    mixed_low = from_items(mixed_items, windows, local, 1)
    resid_one = hidden + jnp.dot(mixed_low, out_mat, preferred_element_type=jnp.float32)
    middle = layer_norm(resid_one, norms[0], norms[1])
    middle_low = middle.astype(jnp.bfloat16)
    pre_gelu = jnp.dot(middle_low, up_mat, preferred_element_type=jnp.float32)
    activated = jax.nn.gelu(pre_gelu, approximate=False).astype(jnp.bfloat16)
    resid_two = middle + jnp.dot(activated, down_mat, preferred_element_type=jnp.float32)
    result = layer_norm(resid_two, norms[2], norms[3])
    return (
        result,
        (
            hidden_low,
            items,
            kept_attn,
            mixed_low,
            resid_one,
            middle_low,
            pre_gelu,
            activated,
            resid_two,
        ),
    )


def layer_backward(dresult, layer_weights, kept, markers, position, group, windows, local):
    joint, out_mat, up_mat, down_mat, norms = layer_weights
    (
        hidden_low,
        items,
        kept_attn,
        mixed_low,
        resid_one,
        middle_low,
        pre_gelu,
        activated,
        resid_two,
    ) = kept
    _, pull_two = jax.vjp(layer_norm, resid_two, norms[2], norms[3])
    dresid_two, dgain_two, dshift_two = pull_two(dresult)
    dbranch = dresid_two.astype(jnp.bfloat16)
    grad_down = jnp.dot(activated.T, dbranch, preferred_element_type=jnp.float32)
    dactive = jnp.dot(dbranch, down_mat.T, preferred_element_type=jnp.float32)
    _, pull_gelu = jax.vjp(partial(jax.nn.gelu, approximate=False), pre_gelu)
    dpre = pull_gelu(dactive)[0].astype(jnp.bfloat16)
    grad_up = jnp.dot(middle_low.T, dpre, preferred_element_type=jnp.float32)
    dmiddle = dresid_two + jnp.dot(dpre, up_mat.T, preferred_element_type=jnp.float32)
    _, pull_one = jax.vjp(layer_norm, resid_one, norms[0], norms[1])
    dresid_one, dgain_one, dshift_one = pull_one(dmiddle)
    dattn = dresid_one.astype(jnp.bfloat16)
    grad_out = jnp.dot(mixed_low.T, dattn, preferred_element_type=jnp.float32)
    mixed_gradient = jnp.dot(dattn, out_mat.T, preferred_element_type=jnp.float32).astype(
        jnp.bfloat16
    )
    ditems = attend_backward(
        items,
        markers,
        to_items(mixed_gradient, windows, local, 1),
        kept_attn,
        position,
        group,
        local,
    )
    dproj = from_items(ditems, windows, local, 3)
    grad_joint = jnp.dot(hidden_low.T, dproj, preferred_element_type=jnp.float32)
    dhidden = dresid_one + jnp.dot(dproj, joint.T, preferred_element_type=jnp.float32)
    grad_norm = jnp.stack([dgain_one, dshift_one, dgain_two, dshift_two])
    return (dhidden, (grad_joint, grad_out, grad_up, grad_down, grad_norm))


def body(
    series,
    target,
    valid_slots,
    observed,
    embed_weight,
    joint_proj,
    out_proj,
    up_proj,
    down_proj,
    head_weight,
    norm_params,
    embed_mean,
    joint_mean,
    out_mean,
    up_mean,
    down_mean,
    head_mean,
    norm_mean,
    embed_square,
    joint_square,
    out_square,
    up_square,
    down_square,
    head_square,
    norm_square,
):
    windows = series.shape[0]
    local = series.shape[1]
    row_count = windows * local
    group = lax.axis_size("win")
    position = lax.axis_index("win")
    embed, joint, out_mat, up_mat, down_mat, head_mat, norms_low = (
        lax.all_gather(embed_weight.astype(jnp.bfloat16), "var", axis=1, tiled=True),
        lax.all_gather(joint_proj.astype(jnp.bfloat16), "var", axis=1, tiled=True),
        lax.all_gather(out_proj.astype(jnp.bfloat16), "var", axis=1, tiled=True),
        lax.all_gather(up_proj.astype(jnp.bfloat16), "var", axis=1, tiled=True),
        lax.all_gather(down_proj.astype(jnp.bfloat16), "var", axis=1, tiled=True),
        lax.all_gather(head_weight.astype(jnp.bfloat16), "var", axis=0, tiled=True),
        lax.all_gather(norm_params.astype(jnp.bfloat16), "var", axis=2, tiled=True),
    )
    norms = norms_low.astype(jnp.float32)
    weight_mask = observed.astype(jnp.float32) * valid_slots.astype(jnp.float32)[None, :, None]
    count = jnp.maximum(lax.psum(jnp.sum(weight_mask), ("var", "win")), 1.0)
    markers = valid_slots.astype(jnp.bfloat16)
    centre = jnp.mean(series, -1, keepdims=True)
    offset = series - centre
    spread = jnp.sqrt(jnp.mean(offset * offset, -1, keepdims=True) + 1e-05)
    normed = (offset / spread).astype(jnp.bfloat16).reshape(row_count, -1)
    hidden = jnp.dot(normed, embed, preferred_element_type=jnp.float32)
    layer = 0
    layer_weights = (joint[layer], out_mat[layer], up_mat[layer], down_mat[layer], norms[layer])
    hidden, kept = layer_forward(hidden, layer_weights, markers, position, group, windows, local)
    kept_layers = [kept]
    final_low = hidden.astype(jnp.bfloat16)
    guess = (
        jnp.dot(final_low, head_mat, preferred_element_type=jnp.float32).reshape(windows, local, -1)
        * spread
        + centre
    )
    error = guess - target
    loss_part = jnp.sum(weight_mask * error * error)
    dguess = (
        (2.0 * weight_mask * error / count * spread).reshape(row_count, -1).astype(jnp.bfloat16)
    )
    grad_head = jnp.dot(final_low.T, dguess, preferred_element_type=jnp.float32)
    dhidden = jnp.dot(dguess, head_mat.T, preferred_element_type=jnp.float32)
    layer_grads = [None] * LAYERS
    for layer in reversed(range(LAYERS)):
        layer_weights = (joint[layer], out_mat[layer], up_mat[layer], down_mat[layer], norms[layer])
        dhidden, layer_grads[layer] = layer_backward(
            dhidden, layer_weights, kept_layers[layer], markers, position, group, windows, local
        )
    grad_embed = jnp.dot(normed.T, dhidden.astype(jnp.bfloat16), preferred_element_type=jnp.float32)
    stacked = [jnp.stack([grads[i] for grads in layer_grads]) for i in range(5)]
    summed = (
        lax.psum_scatter(
            grad_embed.astype(jnp.bfloat16), "var", scatter_dimension=1, tiled=True
        ).astype(jnp.float32),
        lax.psum_scatter(
            stacked[0].astype(jnp.bfloat16), "var", scatter_dimension=1, tiled=True
        ).astype(jnp.float32),
        lax.psum_scatter(
            stacked[1].astype(jnp.bfloat16), "var", scatter_dimension=1, tiled=True
        ).astype(jnp.float32),
        lax.psum_scatter(
            stacked[2].astype(jnp.bfloat16), "var", scatter_dimension=1, tiled=True
        ).astype(jnp.float32),
        lax.psum_scatter(
            stacked[3].astype(jnp.bfloat16), "var", scatter_dimension=1, tiled=True
        ).astype(jnp.float32),
        lax.psum_scatter(
            grad_head.astype(jnp.bfloat16), "var", scatter_dimension=0, tiled=True
        ).astype(jnp.float32),
        lax.psum_scatter(
            stacked[4].astype(jnp.bfloat16), "var", scatter_dimension=2, tiled=True
        ).astype(jnp.float32),
    )
    totals = (
        lax.psum(summed[0].astype(jnp.bfloat16), "win").astype(jnp.float32),
        lax.psum(summed[1].astype(jnp.bfloat16), "win").astype(jnp.float32),
        lax.psum(summed[2].astype(jnp.bfloat16), "win").astype(jnp.float32),
        lax.psum(summed[3].astype(jnp.bfloat16), "win").astype(jnp.float32),
        lax.psum(summed[4].astype(jnp.bfloat16), "win").astype(jnp.float32),
        lax.psum(summed[5].astype(jnp.bfloat16), "win").astype(jnp.float32),
        lax.psum(summed[6].astype(jnp.bfloat16), "win").astype(jnp.float32),
    )
    loss = lax.psum(loss_part, ("var", "win")) / count
    count_step = float(STEP_NUMBER)
    weights = (embed_weight, joint_proj, out_proj, up_proj, down_proj, head_weight, norm_params)
    means = (embed_mean, joint_mean, out_mean, up_mean, down_mean, head_mean, norm_mean)
    squares = (
        embed_square,
        joint_square,
        out_square,
        up_square,
        down_square,
        head_square,
        norm_square,
    )
    results = [adamw(weights[i], means[i], squares[i], totals[i], count_step) for i in range(7)]
    return (
        loss.reshape(1),
        results[0][0],
        results[1][0],
        results[2][0],
        results[3][0],
        results[4][0],
        results[5][0],
        totals[6],
        results[0][1],
        results[1][1],
        results[2][1],
        results[3][1],
        results[4][1],
        results[5][1],
        results[6][1],
        results[0][2],
        results[1][2],
        results[2][2],
        results[3][2],
        results[4][2],
        results[5][2],
        results[6][2],
    )


def solution(mesh):
    placed = (
        P("var", "win", None),
        P("var", "win", None),
        P("win"),
        P("var", "win", None),
        P(None, "var"),
        P(None, "var", None),
        P(None, "var", None),
        P(None, "var", None),
        P(None, "var", None),
        P("var", None),
        P(None, None, "var"),
        P(None, "var"),
        P(None, "var", None),
        P(None, "var", None),
        P(None, "var", None),
        P(None, "var", None),
        P("var", None),
        P(None, None, "var"),
        P(None, "var"),
        P(None, "var", None),
        P(None, "var", None),
        P(None, "var", None),
        P(None, "var", None),
        P("var", None),
        P(None, None, "var"),
    )
    return jax.shard_map(
        body,
        mesh=mesh,
        in_specs=placed,
        out_specs=(
            P(),
            P(None, "var"),
            P(None, "var", None),
            P(None, "var", None),
            P(None, "var", None),
            P(None, "var", None),
            P("var", None),
            P(None, None, "var"),
            P(None, "var"),
            P(None, "var", None),
            P(None, "var", None),
            P(None, "var", None),
            P(None, "var", None),
            P("var", None),
            P(None, None, "var"),
            P(None, "var"),
            P(None, "var", None),
            P(None, "var", None),
            P(None, "var", None),
            P(None, "var", None),
            P("var", None),
            P(None, None, "var"),
        ),
        check_vma=False,
    )
```

profile of v0, /device:TPU:0, one launch (start us, length us, event | category | flops | bytes accessed | tf_op | source)
XLA Modules:
  0.0 1423.5 jit_solution(6629084891601255380)
XLA Ops:
  15.1 23.6 %all_gather.21 = bf16[96,512]{0,1:T(8,128)(2,1)S(1)} all-gather(bf16[96,32]{0,1:T(8,128)(2,1)S(1)} %convert_element_type.207), channel_id=1, replica_groups=mesh['var'=16,'win'=2] {'var'}, dimensions={1}, use_global_device_ids=true | all-gather | bytes 104448 | tf_op jit(solution)/shard_map/all_gather | solution.py:287
  41.2 12.3 all-gather.4.cloned.1.call-done
  53.5 8.0 convolution_convert_fusion
  61.5 8.4 copy.124
  69.9 15.1 %reshape.411 = bf16[4,448,3,8,64]{1,0,4,3,2:T(4,128)(2,1)} reshape(bf16[1792,1536]{0,1:T(8,128)(2,1)} %copy.124) | data formatting | bytes 11010048 | tf_op jit(solution)/shard_map/reshape | solution.py:37
  94.5 6.4 copy.127
  103.9 20.6 %all_gather.24 = bf16[1,4,512]{1,0,2:T(2,128)(2,1)S(1)} all-gather(bf16[1,4,32]{1,0,2:T(2,128)(2,1)S(1)} %copy.132), channel_id=1, replica_groups=mesh['var'=16,'win'=2] {'var'}, dimensions={2}, use_global_device_ids=true | all-gather | bytes 4352 | tf_op jit(solution)/shard_map/all_gather | solution.py:293
  124.9 7.4 slice_reduce_fusion.1
  132.3 19.4 %all_gather.23 = bf16[1,512,512]{2,1,0:T(8,128)(2,1)S(1)} all-gather(bf16[1,32,512]{2,1,0:T(8,128)(2,1)S(1)} %convert_element_type.215), channel_id=1, replica_groups=mesh['var'=16,'win'=2] {'var'}, dimensions={1}, use_global_device_ids=true | all-gather | bytes 557056 | tf_op jit(solution)/shard_map/all_gather | solution.py:289
  151.6 20.9 %all_gather.27 = bf16[512,96]{1,0:T(8,128)(2,1)} all-gather(bf16[32,96]{1,0:T(8,128)(2,1)S(1)} %convert_element_type.223), channel_id=1, replica_groups=mesh['var'=16,'win'=2] {'var'}, dimensions={0}, use_global_device_ids=true | all-gather | bytes 104448 | tf_op jit(solution)/shard_map/all_gather | solution.py:292
  173.1 9.6 collective-permute-done.3
  186.5 14.4 %fusion.13 = (f32[32,448]{1,0:T(8,128)S(1)}, f32[32,448,448]{1,2,0:T(8,128)}) fusion(pred[448,448]{0,1:T(8,128)(4,1)S(1)} %get-tuple-element.469, bf16[32,448,192]{1,2,0:T(8,128)(2,1)} %bitcast.110), kind=kOutput, calls=%fused_computation.24 | convolution fusion | flops 841336832 | bytes 30142464 | tf_op jit(solution)/shard_map/acn,azn->acz/dot_general | solution.py:48
  200.9 13.9 fusion.14
  214.8 14.2 fusion.27
  229.0 23.1 %fusion.15 = (f32[32,448]{1,0:T(8,128)S(1)}, f32[32,448]{1,0:T(8,128)S(1)}) fusion(f32[32,448,448]{1,2,0:T(8,128)} %get-tuple-element.471, f32[32,448]{1,0:T(8,128)S(1)} %get-tuple-element.467, pred[448,448]{0,1:T(8,128)(4,1)S(1)} %get-tuple-element.469, f32[32,448]{1,0:T(8,128)S(1)} %get-tuple-element.466, f32[32,448,448]{1,2,0:T(8,128)} %get-tuple-element.473, ...), kind=kLoop, calls=%fused_computation.26 | loop fusion | flops 51351552 | bytes 52011008 | tf_op jit(solution)/shard_map/reduce_sum | solution.py:63
  252.8 18.7 %fusion.106 = (bf16[32,448,64]{1,2,0:T(8,128)(2,1)}, f32[32,448,64]{1,2,0:T(8,128)}) fusion(f32[32,448]{1,0:T(8,128)S(1)} %get-tuple-element.457, f32[32,448,448]{1,2,0:T(8,128)} %get-tuple-element.473, f32[32,448]{1,0:T(8,128)S(1)} %get-tuple-element.466, pred[448,448]{0,1:T(8,128)(4,1)S(1)} %get-tuple-element.468, ...), kind=kOutput, calls=%fused_computation.184 | convolution fusion | flops 852361216 | bytes 38965248 | tf_op jit(solution)/shard_map/while/body/eval_jaxpr/zsx,zxj->zsj/dot_general | solution.py:65
  287.1 40.9 %multiply_convert_fusion.1 = (bf16[1792,2048]{1,0:T(8,128)(2,1)}, f32[1792,2048]{1,0:T(8,128)}, f32[1792,2048]{1,0:T(8,128)}) fusion(bf16[1,512,2048]{2,1,0:T(8,128)(2,1)} %all-gather.6.cloned.1.call-done, f32[1792,512]{0,1:T(8,128)} %copy-done.5, f32[512]{0:T(512)S(1)} %get-tuple-element.401, f32[512]{0:T(512)S(1)} %get-tuple-element.402, ...), kind=kOutput, calls=%fused_computation.33 | convolution fusion | flops 4001234944 | bytes 42485760 | tf_op jit(solution)/shard_map/dot_general | solution.py:189
  328.0 9.9 fusion.108
  343.3 39.2 %all-reduce = (f32[]{:T(128)}, f32[]{:T(128)}) all-reduce(f32[]{:T(128)} %get-tuple-element.398, f32[]{:T(128)} %get-tuple-element.397), channel_id=1, replica_groups=mesh['var'=16,'win'=2] {'var','win'}, use_global_device_ids=true, to_apply=%region_11.12 | all-reduce | flops 2 | bytes 16 | tf_op jit(solution)/shard_map/psum | solution.py:361
  400.6 18.8 %add_convert_fusion = bf16[1792,2048]{1,0:T(8,128)(2,1)} fusion(f32[1792,2048]{1,0:T(8,128)} %get-tuple-element.462, f32[1792,2048]{1,0:T(8,128)} %get-tuple-element.478, bf16[1,2048,512]{2,1,0:T(8,128)(2,1)} %all-gather.8.cloned.1.call-done, f32[1792,512]{0,1:T(8,128)} %get-tuple-element.460, f32[1792]{0:T(1024)S(1)} %negate_multiply_fusion.2), kind=kOutput, calls=%fused_computation.32 | convolution fusion | flops 3811311616 | bytes 42474496 | tf_op jit(solution)/shard_map/dot_general | solution.py:226
  419.5 10.4 multiply_reduce_fusion.2
  436.4 5.4 reshape.417
  445.8 505.1 %while.14 = (s32[]{:T(128)}, bf16[32,448,128]{2,1,0:T(8,128)(2,1)}, bf16[448]{0:T(512)(128)(2,1)S(1)}, f32[32,448,64]{1,2,0:T(8,128)}, f32[32,448,128]{2,1,0:T(8...) while((s32[]{:T(128)}, bf16[32,448,128]{2,1,0:T(8,128)(2,1)}, ...), condition=%wide.region_20.21_spmd.clone, body=%wide.region_19.20_spmd.clone.sunk | while | flops 4187890944 | bytes 271890912 | solution.py:171
  450.3 6.4 copy.170
  456.8 15.4 %fusion.158 = f32[32,448,448]{2,1,0:T(8,128)} fusion(bf16[32,448,64]{1,2,0:T(8,128)(2,1)S(1)} %get-tuple-element.589, bf16[32,448,128]{1,2,0:T(8,128)(2,1)} %copy.170), kind=kOutput, calls=%fused_computation.12.clone.1 | convolution fusion | flops 822083584 | bytes 29622272 | tf_op jit(solution)/shard_map/while/body/eval_jaxpr/acn,azn->acz/dot_general | solution.py:48
  472.4 14.5 %fusion.159 = f32[32,448,64]{1,2,0:T(8,128)} fusion(bf16[32,448,64]{1,2,0:T(8,128)(2,1)S(1)} %copy-done.14, f32[32,448,448]{2,1,0:T(8,128)} %fusion.158, f32[32,448]{1,0:T(8,128)S(1)} %get-tuple-element.590, pred[448,448]{1,0:T(8,128)(4,1)S(1)} %compare_or_fusion.4), kind=kOutput, calls=%fused_computation.4.clone.1 | convolution fusion | flops 847773696 | bytes 31453184 | tf_op jit(solution)/shard_map/while/body/eval_jaxpr/fov,foc->fvc/dot_general | solution.py:97
  486.9 19.1 %multiply_convert_fusion.4 = bf16[32,448,448]{2,1,0:T(8,128)(2,1)} fusion(f32[32,448,448]{2,1,0:T(8,128)} %fusion.158, f32[32,448]{1,0:T(8,128)S(1)} %get-tuple-element.592, f32[32,448]{1,0:T(8,128)S(1)} %get-tuple-element.590, pred[448,448]{1,0:T(8,128)(4,1)S(1)} %compare_or_fusion.4, bf16[32,448,64]{1,2,0:T(8,128)(2,1)} %get-tuple-element.591, ...), kind=kOutput, calls=%fused_computation.1.clone.1 | convolution fusion | flops 860618752 | bytes 42827776 | tf_op jit(solution)/shard_map/while/body/eval_jaxpr/acn,azn->acz/dot_general | solution.py:81
  506.0 10.5 convolution_multiply_fusion.2
  516.5 9.0 copy.171
  525.6 6.0 fusion.160
  531.6 6.3 copy.172
  542.2 10.7 select_add_fusion.2
  552.9 67.8 %collective-permute-done.2 = bf16[32,448,128]{2,1,0:T(8,128)(2,1)} collective-permute-done((bf16[32,448,128]{2,1,0:T(8,128)(2,1)}, bf16[32,448,128]{2,1,0:T(8,128)(2,1)}, u32[]{:S(2)}, u32[]{:S(2)}) %collective-permute-start.2) | collective-permute-done | bytes 3670048 | tf_op jit(solution)/shard_map/while/body/eval_jaxpr/ppermute | solution.py:17
  620.8 5.8 convert_element_type.373
  626.6 70.9 %collective-permute-done.1 = bf16[448]{0:T(512)(128)(2,1)S(1)} collective-permute-done((bf16[448]{0:T(512)(128)(2,1)S(1)}, bf16[448]{0:T(512)(128)(2,1)S(1)}, u32[]{:S(2)}, u32[]{:S(2)}) %collective-permute-start.1) | collective-permute-done | bytes 928 | tf_op jit(solution)/shard_map/while/body/eval_jaxpr/ppermute | solution.py:17
  701.8 6.4 copy.170
  708.2 15.4 %fusion.158 = f32[32,448,448]{2,1,0:T(8,128)} fusion(bf16[32,448,64]{1,2,0:T(8,128)(2,1)S(1)} %get-tuple-element.589, bf16[32,448,128]{1,2,0:T(8,128)(2,1)} %copy.170), kind=kOutput, calls=%fused_computation.12.clone.1 | convolution fusion | flops 822083584 | bytes 29622272 | tf_op jit(solution)/shard_map/while/body/eval_jaxpr/acn,azn->acz/dot_general | solution.py:48
  723.9 14.5 %fusion.159 = f32[32,448,64]{1,2,0:T(8,128)} fusion(bf16[32,448,64]{1,2,0:T(8,128)(2,1)S(1)} %copy-done.14, f32[32,448,448]{2,1,0:T(8,128)} %fusion.158, f32[32,448]{1,0:T(8,128)S(1)} %get-tuple-element.590, pred[448,448]{1,0:T(8,128)(4,1)S(1)} %compare_or_fusion.4), kind=kOutput, calls=%fused_computation.4.clone.1 | convolution fusion | flops 847773696 | bytes 31453184 | tf_op jit(solution)/shard_map/while/body/eval_jaxpr/fov,foc->fvc/dot_general | solution.py:97
  738.4 19.1 %multiply_convert_fusion.4 = bf16[32,448,448]{2,1,0:T(8,128)(2,1)} fusion(f32[32,448,448]{2,1,0:T(8,128)} %fusion.158, f32[32,448]{1,0:T(8,128)S(1)} %get-tuple-element.592, f32[32,448]{1,0:T(8,128)S(1)} %get-tuple-element.590, pred[448,448]{1,0:T(8,128)(4,1)S(1)} %compare_or_fusion.4, bf16[32,448,64]{1,2,0:T(8,128)(2,1)} %get-tuple-element.591, ...), kind=kOutput, calls=%fused_computation.1.clone.1 | convolution fusion | flops 860618752 | bytes 42827776 | tf_op jit(solution)/shard_map/while/body/eval_jaxpr/acn,azn->acz/dot_general | solution.py:81
  757.5 10.5 convolution_multiply_fusion.2
  768.0 9.0 copy.171
  777.0 8.8 fusion.160
  785.8 6.3 copy.172
  795.9 11.3 select_add_fusion.2
  807.2 67.5 %collective-permute-done.2 = bf16[32,448,128]{2,1,0:T(8,128)(2,1)} collective-permute-done((bf16[32,448,128]{2,1,0:T(8,128)(2,1)}, bf16[32,448,128]{2,1,0:T(8,128)(2,1)}, u32[]{:S(2)}, u32[]{:S(2)}) %collective-permute-start.2) | collective-permute-done | bytes 3670048 | tf_op jit(solution)/shard_map/while/body/eval_jaxpr/ppermute | solution.py:17
  874.7 5.8 convert_element_type.373
  880.5 70.0 %collective-permute-done.1 = bf16[448]{0:T(512)(128)(2,1)S(1)} collective-permute-done((bf16[448]{0:T(512)(128)(2,1)S(1)}, bf16[448]{0:T(512)(128)(2,1)S(1)}, u32[]{:S(2)}, u32[]{:S(2)}) %collective-permute-start.1) | collective-permute-done | bytes 928 | tf_op jit(solution)/shard_map/while/body/eval_jaxpr/ppermute | solution.py:17
  950.9 5.5 convert.23
  962.6 9.0 pad_maximum_fusion
  972.9 10.4 copy.141
  983.3 11.2 copy.142
  994.5 12.6 reshape.419
  1007.2 8.5 fusion.52
  1020.1 7.9 fusion.35
  1028.1 9.6 fusion.37
  1038.0 9.7 fusion.36
  1049.4 25.8 %reduce-scatter.20.cloned.1.call-done = bf16[32,96]{1,0:T(8,128)(2,1)} async-done(((bf16[512,96]{1,0:T(8,128)(2,1)}), bf16[32,96]{1,0:T(8,128)(2,1)}) %reduce-scatter.20.cloned.1.call-update) | async-done | bytes 6160 | tf_op jit(solution)/shard_map/reduce_scatter | solution.py:345
  1075.2 58.0 %reduce-scatter.10.cloned.1.call-done = bf16[96,32]{0,1:T(8,128)(2,1)} async-done(((bf16[96,512]{0,1:T(8,128)(2,1)}), bf16[96,32]{0,1:T(8,128)(2,1)}) %reduce-scatter.10.cloned.1.call-update) | async-done | bytes 6160 | tf_op jit(solution)/shard_map/reduce_scatter | solution.py:330
  1133.2 58.4 %reduce-scatter.14.cloned.1.call-done = bf16[1,32,512]{2,1,0:T(8,128)(2,1)} async-done(((bf16[1,512,512]{2,1,0:T(8,128)(2,1)}), bf16[1,32,512]{2,1,0:T(8,128)(2,1)}) %reduce-scatter.14.cloned.1.call-update) | async-done | bytes 32784 | tf_op jit(solution)/shard_map/reduce_scatter | solution.py:336
  1191.5 9.3 all-reduce.1
  1202.8 51.5 %reduce-scatter.12.cloned.1.call-done = bf16[1,32,1536]{2,1,0:T(8,128)(2,1)} async-done(((bf16[1,512,1536]{2,1,0:T(8,128)(2,1)}), bf16[1,32,1536]{2,1,0:T(8,128)(2,1)}) %reduce-scatter.12.cloned.1.call-update) | async-done | bytes 98320 | tf_op jit(solution)/shard_map/reduce_scatter | solution.py:333
  1254.2 64.3 %reduce-scatter.18.cloned.1.call-done = bf16[1,128,512]{2,1,0:T(8,128)(2,1)} async-done(((bf16[1,2048,512]{2,1,0:T(8,128)(2,1)}), bf16[1,128,512]{2,1,0:T(8,128)(2,1)}) %reduce-scatter.18.cloned.1.call-update) | async-done | bytes 131088 | tf_op jit(solution)/shard_map/reduce_scatter | solution.py:342
  1318.6 64.7 %reduce-scatter.16.cloned.1.call-done = bf16[1,32,2048]{2,1,0:T(8,128)(2,1)} async-done(((bf16[1,512,2048]{2,1,0:T(8,128)(2,1)}), bf16[1,32,2048]{2,1,0:T(8,128)(2,1)}) %reduce-scatter.16.cloned.1.call-update) | async-done | bytes 131088 | tf_op jit(solution)/shard_map/reduce_scatter | solution.py:339
  1384.6 25.5 %all-reduce.5.cloned.1.call-done = (bf16[1,32,1536]{2,1,0:T(8,128)(2,1)}, bf16[1,32,2048]{2,1,0:T(8,128)(2,1)}, bf16[1,128,512]{2,1,0:T(8,128)(2,1)}) async-done(((bf16[1,32,1536]{2,1,0:T(8,128)(2,1)}, bf16[1,32,2048]{2,1,0:T(8,128)(2,1)}, bf16[1,128,512]{2,1,0:T(8,128)(2,1)}), (bf16[1,32,1536]{2,1,0:T(8,128)(2,1)}, bf16[1,32,2048]{2,1,0:T(8,128)(2,1)}, ...) | async-done | bytes 360464 | tf_op jit(solution)/shard_map/psum | solution.py:354
  (302 shorter events, 115.4 us)
Async XLA Ops:
  7.2 46.3 %all-gather.4.cloned.1.call-start = ((), (), s32[]{:S(2)}) async-start(), calls=%async_computation.7 | async-start | bytes 1671168 | tf_op jit(solution)/shard_map/all_gather | solution.py:288
  8.9 278.2 %all-gather.6.cloned.1.call-start = ((), (), s32[]{:S(2)}) async-start(), calls=%async_computation.8 | async-start | bytes 2228224 | tf_op jit(solution)/shard_map/all_gather | solution.py:290
  10.5 317.4 %all-gather.8.cloned.1.call-start = ((), (), s32[]{:S(2)}) async-start(), calls=%async_computation.9 | async-start | bytes 2228224 | tf_op jit(solution)/shard_map/all_gather | solution.py:291
  15.1 46.4 %copy-start.23 = (bf16[1792,96]{0,1:T(8,128)(2,1)}, bf16[1792,96]{0,1:T(8,128)(2,1)S(1)}, u32[]{:S(2)}) copy-start(bf16[1792,96]{0,1:T(8,128)(2,1)S(1)} %reshape.410) | copy-start | bytes 1032196
  94.5 30.3 %copy-start.47 = (f32[32,96]{1,0:T(8,128)S(1)}, f32[32,96]{1,0:T(8,128)}, u32[]{:S(2)}) copy-start(f32[32,96]{1,0:T(8,128)} %param.36) | copy-start | bytes 36868
  100.9 100.0 %collective-permute-start.4 = (bf16[32,448,128]{2,1,0:T(8,128)(2,1)}, bf16[32,448,128]{2,1,0:T(8,128)(2,1)}, u32[]{:S(2)}, u32[]{:S(2)}) collective-permute-start(bf16[32,448,128]{2,1,0:T(8,128)(2,1)} %copy.127), channel_id=1, source_target_pairs={{1,0},{0,1},{3,2},{2,3},{5,4},{4,5},{7,6},{6,7},{9,8},{8,9},{11,10... | collective-permute-start | bytes 11010056 | tf_op jit(solution)/shard_map/while/body/eval_jaxpr/ppermute | solution.py:17
  102.5 84.0 %copy-start.53 = (bf16[448]{0:T(512)(128)(2,1)}, bf16[448]{0:T(512)(128)(2,1)S(1)}, u32[]{:S(2)}) copy-start(bf16[448]{0:T(512)(128)(2,1)S(1)} %get-tuple-element.555) | copy-start | bytes 2692
  102.5 80.3 %collective-permute-start.3 = (bf16[448]{0:T(512)(128)(2,1)S(1)}, bf16[448]{0:T(512)(128)(2,1)S(1)}, u32[]{:S(2)}, u32[]{:S(2)}) collective-permute-start(bf16[448]{0:T(512)(128)(2,1)S(1)} %get-tuple-element.555), channel_id=1, source_target_pairs={{1,0},{0,1},{3,2},{2,3},{5,4},{4,5},{7,6},{6,7},{9,8},{8,9},{11,10... | collective-permute-start | bytes 2696 | tf_op jit(solution)/shard_map/while/body/eval_jaxpr/ppermute | solution.py:17
  103.7 944.8 %reduce-scatter.22.cloned.1.call-start = ((), (), s32[]{:S(2)}) async-start(), calls=%async_computation.16 | async-start | bytes 139264
  132.3 195.7 %copy-start.74 = (f32[512]{0:T(512)}, f32[512]{0:T(512)S(1)}, u32[]{:S(2)}) copy-start(f32[512]{0:T(512)S(1)} %get-tuple-element.401) | copy-start | bytes 6148
  132.3 297.6 %copy-start.63 = (f32[512]{0:T(512)}, f32[512]{0:T(512)S(1)}, u32[]{:S(2)}) copy-start(f32[512]{0:T(512)S(1)} %get-tuple-element.402) | copy-start | bytes 6148
  151.6 128.6 %copy-start.21 = (bf16[1,512,512]{2,1,0:T(8,128)(2,1)}, bf16[1,512,512]{2,1,0:T(8,128)(2,1)S(1)}, u32[]{:S(2)}) copy-start(bf16[1,512,512]{2,1,0:T(8,128)(2,1)S(1)} %all_gather.23) | copy-start | bytes 1572868
  183.2 17.7 %slice-start = ((s8[6291456]{0:T(1024)(128)(4,1)}), s8[4194304]{0:T(1024)(128)(4,1)S(1)}, s32[]{:S(2)}) async-start(s8[6291456]{0:T(1024)(128)(4,1)} %bitcast.111), calls=%async_computation.18 | async-start | bytes 8388608
  186.5 14.4 %slice-start.1 = ((s8[6291456]{0:T(1024)(128)(4,1)}), s8[2097152]{0:T(1024)(128)(4,1)S(1)}, s32[]{:S(2)}) async-start(s8[6291456]{0:T(1024)(128)(4,1)} %bitcast.111), calls=%async_computation.19 | async-start | bytes 4194304
  284.2 145.7 %copy-start.42 = (f32[1792]{0:T(1024)}, f32[1792]{0:T(1024)S(1)}, u32[]{:S(2)}) copy-start(f32[1792]{0:T(1024)S(1)} %broadcast_multiply_fusion.1) | copy-start | bytes 21508
  287.0 142.9 %copy-start.56 = (f32[1792]{0:T(1024)}, f32[1792]{0:T(1024)S(1)}, u32[]{:S(2)}) copy-start(f32[1792]{0:T(1024)S(1)} %fusion.75) | copy-start | bytes 21508
  328.0 10.4 copy-start.55
  328.0 10.4 copy-start.65
  400.6 18.8 %copy-start.68 = (f32[1792]{0:T(1024)}, f32[1792]{0:T(1024)S(1)}, u32[]{:S(2)}) copy-start(f32[1792]{0:T(1024)S(1)} %negate_multiply_fusion.2) | copy-start | bytes 21508
  400.6 18.8 %copy-start.81 = (bf16[1,512,2048]{2,1,0:T(8,128)(2,1)S(1)}, bf16[1,512,2048]{2,1,0:T(8,128)(2,1)}, u32[]{:S(2)}) copy-start(bf16[1,512,2048]{2,1,0:T(8,128)(2,1)} %all-gather.6.cloned.1.call-done) | copy-start | bytes 6291460
  419.5 10.4 copy-start.45
  419.5 10.5 copy-start.6
  456.8 15.7 %copy-start.14 = (bf16[32,448,64]{1,2,0:T(8,128)(2,1)S(1)}, bf16[32,448,64]{1,2,0:T(8,128)(2,1)}, u32[]{:S(2)}) copy-start(bf16[32,448,64]{1,2,0:T(8,128)(2,1)} %get-tuple-element.591) | copy-start | bytes 5505028 | tf_op jit(solution)/shard_map/while
  472.4 14.5 %copy-start = (bf16[32,448,128]{1,2,0:T(8,128)(2,1)S(1)}, bf16[32,448,128]{1,2,0:T(8,128)(2,1)}, u32[]{:S(2)}) copy-start(bf16[32,448,128]{1,2,0:T(8,128)(2,1)} %copy.170) | copy-start | bytes 11010052 | tf_op jit(solution)/shard_map/while
  537.9 82.8 %collective-permute-start.2 = (bf16[32,448,128]{2,1,0:T(8,128)(2,1)}, bf16[32,448,128]{2,1,0:T(8,128)(2,1)}, u32[]{:S(2)}, u32[]{:S(2)}) collective-permute-start(bf16[32,448,128]{2,1,0:T(8,128)(2,1)} %copy.172), channel_id=1, source_target_pairs={{1,0},{0,1},{3,2},{2,3},{5,4},{4,5},{7,6},{6,7},{9,8},{8,9},{11,10... | collective-permute-start | bytes 11010056 | tf_op jit(solution)/shard_map/while/body/eval_jaxpr/ppermute | solution.py:17
  540.2 157.3 %collective-permute-start = (bf16[32,448,128]{2,1,0:T(8,128)(2,1)}, bf16[32,448,128]{2,1,0:T(8,128)(2,1)}, u32[]{:S(2)}, u32[]{:S(2)}) collective-permute-start(bf16[32,448,128]{2,1,0:T(8,128)(2,1)} %copy.179), channel_id=1, source_target_pairs={{1,0},{0,1},{3,2},{2,3},{5,4},{4,5},{7,6},{6,7},{9,8},{8,9},{11,10... | collective-permute-start | bytes 11010056 | tf_op jit(solution)/shard_map/while/body/eval_jaxpr/ppermute | solution.py:17
  540.2 157.2 %collective-permute-start.1 = (bf16[448]{0:T(512)(128)(2,1)S(1)}, bf16[448]{0:T(512)(128)(2,1)S(1)}, u32[]{:S(2)}, u32[]{:S(2)}) collective-permute-start(bf16[448]{0:T(512)(128)(2,1)S(1)} %copy.180), channel_id=1, source_target_pairs={{1,0},{0,1},{3,2},{2,3},{5,4},{4,5},{7,6},{6,7},{9,8},{8,9},{11,10... | collective-permute-start | bytes 2696 | tf_op jit(solution)/shard_map/while/body/eval_jaxpr/ppermute | solution.py:17
  552.9 144.6 %copy-start.2 = (bf16[32,448,64]{1,2,0:T(8,128)(2,1)S(1)}, bf16[32,448,64]{1,2,0:T(8,128)(2,1)}, u32[]{:S(2)}) copy-start(bf16[32,448,64]{1,2,0:T(8,128)(2,1)} %get-tuple-element.630) | copy-start | bytes 5505028 | tf_op jit(solution)/shard_map/while
  708.2 15.7 %copy-start.14 = (bf16[32,448,64]{1,2,0:T(8,128)(2,1)S(1)}, bf16[32,448,64]{1,2,0:T(8,128)(2,1)}, u32[]{:S(2)}) copy-start(bf16[32,448,64]{1,2,0:T(8,128)(2,1)} %get-tuple-element.591) | copy-start | bytes 5505028 | tf_op jit(solution)/shard_map/while
  723.9 14.5 %copy-start = (bf16[32,448,128]{1,2,0:T(8,128)(2,1)S(1)}, bf16[32,448,128]{1,2,0:T(8,128)(2,1)}, u32[]{:S(2)}) copy-start(bf16[32,448,128]{1,2,0:T(8,128)(2,1)} %copy.170) | copy-start | bytes 11010052 | tf_op jit(solution)/shard_map/while
  792.1 82.6 %collective-permute-start.2 = (bf16[32,448,128]{2,1,0:T(8,128)(2,1)}, bf16[32,448,128]{2,1,0:T(8,128)(2,1)}, u32[]{:S(2)}, u32[]{:S(2)}) collective-permute-start(bf16[32,448,128]{2,1,0:T(8,128)(2,1)} %copy.172), channel_id=1, source_target_pairs={{1,0},{0,1},{3,2},{2,3},{5,4},{4,5},{7,6},{6,7},{9,8},{8,9},{11,10... | collective-permute-start | bytes 11010056 | tf_op jit(solution)/shard_map/while/body/eval_jaxpr/ppermute | solution.py:17
  793.9 156.6 %collective-permute-start = (bf16[32,448,128]{2,1,0:T(8,128)(2,1)}, bf16[32,448,128]{2,1,0:T(8,128)(2,1)}, u32[]{:S(2)}, u32[]{:S(2)}) collective-permute-start(bf16[32,448,128]{2,1,0:T(8,128)(2,1)} %copy.179), channel_id=1, source_target_pairs={{1,0},{0,1},{3,2},{2,3},{5,4},{4,5},{7,6},{6,7},{9,8},{8,9},{11,10... | collective-permute-start | bytes 11010056 | tf_op jit(solution)/shard_map/while/body/eval_jaxpr/ppermute | solution.py:17
  794.2 156.4 %collective-permute-start.1 = (bf16[448]{0:T(512)(128)(2,1)S(1)}, bf16[448]{0:T(512)(128)(2,1)S(1)}, u32[]{:S(2)}, u32[]{:S(2)}) collective-permute-start(bf16[448]{0:T(512)(128)(2,1)S(1)} %copy.180), channel_id=1, source_target_pairs={{1,0},{0,1},{3,2},{2,3},{5,4},{4,5},{7,6},{6,7},{9,8},{8,9},{11,10... | collective-permute-start | bytes 2696 | tf_op jit(solution)/shard_map/while/body/eval_jaxpr/ppermute | solution.py:17
  807.2 143.3 %copy-start.2 = (bf16[32,448,64]{1,2,0:T(8,128)(2,1)S(1)}, bf16[32,448,64]{1,2,0:T(8,128)(2,1)}, u32[]{:S(2)}) copy-start(bf16[32,448,64]{1,2,0:T(8,128)(2,1)} %get-tuple-element.630) | copy-start | bytes 5505028 | tf_op jit(solution)/shard_map/while
  962.6 112.6 %reduce-scatter.20.cloned.1.call-start = ((), (), s32[]{:S(2)}) async-start(), calls=%async_computation.15 | async-start | bytes 139264 | tf_op jit(solution)/shard_map/reduce_scatter | solution.py:345
  994.5 12.7 copy-start.24
  994.5 12.7 copy-start.71
  1007.1 126.1 %reduce-scatter.10.cloned.1.call-start = ((), (), s32[]{:S(2)}) async-start(), calls=%async_computation.10 | async-start | bytes 139264 | tf_op jit(solution)/shard_map/reduce_scatter | solution.py:330
  1015.7 175.8 %reduce-scatter.14.cloned.1.call-start = ((), (), s32[]{:S(2)}) async-start(), calls=%async_computation.12 | async-start | bytes 557056 | tf_op jit(solution)/shard_map/reduce_scatter | solution.py:336
  1019.8 234.4 %reduce-scatter.12.cloned.1.call-start = ((), (), s32[]{:S(2)}) async-start(), calls=%async_computation.11 | async-start | bytes 1671168 | tf_op jit(solution)/shard_map/reduce_scatter | solution.py:333
  1028.0 290.5 %reduce-scatter.18.cloned.1.call-start = ((), (), s32[]{:S(2)}) async-start(), calls=%async_computation.14 | async-start | bytes 2228224 | tf_op jit(solution)/shard_map/reduce_scatter | solution.py:342
  1037.7 163.1 %copy-start.76 = (f32[1,4,32]{2,1,0:T(4,128)S(1)}, f32[1,4,32]{2,1,0:T(4,128)}, u32[]{:S(2)}) copy-start(f32[1,4,32]{2,1,0:T(4,128)} %param.51) | copy-start | bytes 1540
  1037.7 163.7 %copy-start.48 = (f32[32,96]{1,0:T(8,128)S(1)}, f32[32,96]{1,0:T(8,128)}, u32[]{:S(2)}) copy-start(f32[32,96]{1,0:T(8,128)} %param.36) | copy-start | bytes 36868
  1037.7 163.7 %copy-start.59 = (f32[32,96]{1,0:T(8,128)S(1)}, f32[32,96]{1,0:T(8,128)}, u32[]{:S(2)}) copy-start(f32[32,96]{1,0:T(8,128)} %param.43) | copy-start | bytes 36868
  1037.8 163.7 %copy-start.60 = (f32[32,96]{1,0:T(8,128)S(1)}, f32[32,96]{1,0:T(8,128)}, u32[]{:S(2)}) copy-start(f32[32,96]{1,0:T(8,128)} %param.50) | copy-start | bytes 36868
  1037.8 164.3 %copy-start.50 = (f32[96,32]{0,1:T(8,128)S(1)}, f32[96,32]{0,1:T(8,128)}, u32[]{:S(2)}) copy-start(f32[96,32]{0,1:T(8,128)} %param.31) | copy-start | bytes 36868
  1037.8 164.3 %copy-start.61 = (f32[96,32]{0,1:T(8,128)S(1)}, f32[96,32]{0,1:T(8,128)}, u32[]{:S(2)}) copy-start(f32[96,32]{0,1:T(8,128)} %param.38) | copy-start | bytes 36868
  1037.8 164.3 %copy-start.62 = (f32[96,32]{0,1:T(8,128)S(1)}, f32[96,32]{0,1:T(8,128)}, u32[]{:S(2)}) copy-start(f32[96,32]{0,1:T(8,128)} %param.45) | copy-start | bytes 36868
  1037.8 345.5 %copy-start.77 = (f32[1,4,32]{2,1,0:T(4,128)S(1)}, f32[1,4,32]{2,1,0:T(4,128)}, u32[]{:S(2)}) copy-start(f32[1,4,32]{2,1,0:T(4,128)} %param.44) | copy-start | bytes 1540
  1037.8 346.1 %copy-start.31 = (f32[1,32,512]{2,1,0:T(8,128)S(1)}, f32[1,32,512]{2,1,0:T(8,128)}, u32[]{:S(2)}) copy-start(f32[1,32,512]{2,1,0:T(8,128)} %param.33) | copy-start | bytes 196612
  1037.8 346.0 %copy-start.51 = (f32[1,32,512]{2,1,0:T(8,128)S(1)}, f32[1,32,512]{2,1,0:T(8,128)}, u32[]{:S(2)}) copy-start(f32[1,32,512]{2,1,0:T(8,128)} %param.40) | copy-start | bytes 196612
  1037.8 346.0 %copy-start.52 = (f32[1,32,512]{2,1,0:T(8,128)S(1)}, f32[1,32,512]{2,1,0:T(8,128)}, u32[]{:S(2)}) copy-start(f32[1,32,512]{2,1,0:T(8,128)} %param.47) | copy-start | bytes 196612
  1037.9 372.2 %copy-start.27 = (f32[1,128,512]{2,1,0:T(8,128)S(1)}, f32[1,128,512]{2,1,0:T(8,128)}, u32[]{:S(2)}) copy-start(f32[1,128,512]{2,1,0:T(8,128)} %param.35) | copy-start | bytes 786436
  1037.9 372.2 %copy-start.32 = (f32[1,128,512]{2,1,0:T(8,128)S(1)}, f32[1,128,512]{2,1,0:T(8,128)}, u32[]{:S(2)}) copy-start(f32[1,128,512]{2,1,0:T(8,128)} %param.42) | copy-start | bytes 786436
  1037.9 372.2 %copy-start.33 = (f32[1,128,512]{2,1,0:T(8,128)S(1)}, f32[1,128,512]{2,1,0:T(8,128)}, u32[]{:S(2)}) copy-start(f32[1,128,512]{2,1,0:T(8,128)} %param.49) | copy-start | bytes 786436
  1037.9 345.4 %reduce-scatter.16.cloned.1.call-start = ((), (), s32[]{:S(2)}) async-start(), calls=%async_computation.13 | async-start | bytes 2228224 | tf_op jit(solution)/shard_map/reduce_scatter | solution.py:339
  1047.7 364.3 %copy-start.28 = (f32[1,32,2048]{2,1,0:T(8,128)S(1)}, f32[1,32,2048]{2,1,0:T(8,128)}, u32[]{:S(2)}) copy-start(f32[1,32,2048]{2,1,0:T(8,128)} %param.34) | copy-start | bytes 786436
  1047.7 364.3 %copy-start.34 = (f32[1,32,2048]{2,1,0:T(8,128)S(1)}, f32[1,32,2048]{2,1,0:T(8,128)}, u32[]{:S(2)}) copy-start(f32[1,32,2048]{2,1,0:T(8,128)} %param.41) | copy-start | bytes 786436
  1047.7 364.3 %copy-start.35 = (f32[1,32,2048]{2,1,0:T(8,128)S(1)}, f32[1,32,2048]{2,1,0:T(8,128)}, u32[]{:S(2)}) copy-start(f32[1,32,2048]{2,1,0:T(8,128)} %param.48) | copy-start | bytes 786436
  1047.7 366.2 %copy-start.29 = (f32[1,32,1536]{2,1,0:T(8,128)S(1)}, f32[1,32,1536]{2,1,0:T(8,128)}, u32[]{:S(2)}) copy-start(f32[1,32,1536]{2,1,0:T(8,128)} %param.32) | copy-start | bytes 589828
  1047.7 366.2 %copy-start.38 = (f32[1,32,1536]{2,1,0:T(8,128)S(1)}, f32[1,32,1536]{2,1,0:T(8,128)}, u32[]{:S(2)}) copy-start(f32[1,32,1536]{2,1,0:T(8,128)} %param.39) | copy-start | bytes 589828
  1047.7 366.2 %copy-start.39 = (f32[1,32,1536]{2,1,0:T(8,128)S(1)}, f32[1,32,1536]{2,1,0:T(8,128)}, u32[]{:S(2)}) copy-start(f32[1,32,1536]{2,1,0:T(8,128)} %param.46) | copy-start | bytes 589828
  1047.7 362.3 %all-reduce.5.cloned.1.call-start = ((), (), s32[]{:S(2)}) async-start(), calls=%async_computation.17 | async-start | bytes 720896 | tf_op jit(solution)/shard_map/psum | solution.py:354
  1201.5 214.2 %copy-start.66 = (f32[1,4,32]{2,1,0:T(4,128)}, f32[1,4,32]{2,1,0:T(4,128)S(1)}, u32[]{:S(2)}) copy-start(f32[1,4,32]{2,1,0:T(4,128)S(1)} %get-tuple-element.435) | copy-start | bytes 1540
  (42 other events, 219.9 us)
Sparse Core Ops, SparseCore 0:
  10.9 42.5 all-gather.3
  56.2 40.2 all-gather.5
  103.8 41.4 all-gather.7
  962.7 54.4 reduce-scatter.21
  1021.1 54.0 reduce-scatter.19
  1079.1 54.0 reduce-scatter.9
  1136.7 54.7 reduce-scatter.13
  1195.6 58.5 reduce-scatter.11
  1258.0 60.5 reduce-scatter.17
  1322.6 60.6 reduce-scatter.15
  1385.7 24.3 all-reduce.4
where the time goes:
time: 1430 us; the launch traced here: 1420 us
  waiting for transfers between devices  647 us (45%)
  matrix products  342 us (24%)
  local copies, waits for them, and re-layouts  177 us (12%)
  blocking collectives  133 us (9%)
  other arithmetic  95.2 us (7%)
  between operations  17.8 us (1%)
    ppermute x8, waiting for transfers between devices, passed_along(): return lax.ppermute(block, axis, route)  286 us
    reduce_scatter x1, waiting for transfers between devices, body(): lax.psum_scatter(stacked[2].astype(jnp.bfloat16), 'var', scatter_dimensio...  64.7 us
    reduce_scatter x1, waiting for transfers between devices, body(): lax.psum_scatter(stacked[3].astype(jnp.bfloat16), 'var', scatter_dimensio...  64.3 us
    dot_general x4, matrix products, masked_scores(): jnp.einsum('acn,azn->acz', query_rows, key_portion, preferred_element_typ...  59.1 us
    reduce_scatter x1, waiting for transfers between devices, body(): lax.psum_scatter(stacked[1].astype(jnp.bfloat16), 'var', scatter_dimensio...  58.4 us
    reduce_scatter x1, waiting for transfers between devices, body(): lax.psum_scatter(grad_embed.astype(jnp.bfloat16), 'var', scatter_dimensio...  58 us
    reduce_scatter x1, waiting for transfers between devices, body(): lax.psum_scatter(stacked[0].astype(jnp.bfloat16), 'var', scatter_dimensio...  51.5 us
    dot_general x1, matrix products, layer_forward(): pre_gelu = jnp.dot(middle_low, up_mat, preferred_element_type=jnp.float32)  40.9 us
  transfers between devices with their start and end apart: 19, of which 13 were waited for; matrix products, arithmetic and copies ran while one was open for 23% of the time, Pallas kernels for 0%

commit v1 on v0

--- a/solution.py
+++ b/solution.py
@@ -3,6 +3,8 @@
 import jax
 import jax.numpy as jnp
 from jax import lax
+from jax.experimental import pallas as pl
+from jax.experimental.pallas import tpu as pltpu
 from jax.sharding import PartitionSpec as P
 
 HEADS = 8
@@ -10,18 +12,740 @@
 LAYERS = 1
 STEP_NUMBER = 10
 
-
-def passed_along(block, axis, distance):
-    devices = range(lax.axis_size(axis))
-    route = [((i - distance) % len(devices), i) for i in devices]
-    return lax.ppermute(block, axis, route)
-
-
-def layer_norm(resid, gain, shift):
-    centre = jnp.mean(resid, -1, keepdims=True)
+F32 = jnp.float32
+BF16 = jnp.bfloat16
+LANES = 128
+D = HEADS * HEAD_SIZE
+PARTS = 16
+ROWS = D // PARTS
+MIB = 1 << 20
+
+OUT_AT, UP_AT, DOWN_AT, HEAD_AT, LOSS_AT, BUNDLE = 0, 128, 640, 1152, 1184, 1200
+EMBED_AT, FIRST = 384, 416
+
+
+def dot_nn(a, b):
+    return lax.dot_general(a, b, (((1,), (0,)), ((), ())), preferred_element_type=F32)
+
+
+def dot_nt(a, b):
+    return lax.dot_general(a, b, (((1,), (1,)), ((), ())), preferred_element_type=F32)
+
+
+def dot_tn(a, b):
+    return lax.dot_general(a, b, (((0,), (0,)), ((), ())), preferred_element_type=F32)
+
+
+def offset_of(slot):
+    return (slot % 4) * 4 + (slot // 4 % 2) * 2 + slot // 8
+
+
+def slot_of(offset):
+    return (offset & 1) * 8 + ((offset >> 1) & 1) * 4 + (offset >> 2)
+
+
+def lane_index(shape):
+    return lax.broadcasted_iota(jnp.int32, shape, len(shape) - 1)
+
+
+def params(limit=56, **more):
+    return pltpu.CompilerParams(vmem_limit_bytes=limit * MIB, **more)
+
+
+def cost(flops, moved):
+    return pl.CostEstimate(flops=int(flops), bytes_accessed=int(moved), transcendentals=0)
+
+
+def swapped(block, axis, distance):
+    count = lax.axis_size(axis)
+    return lax.ppermute(block, axis, [(i, i ^ distance) for i in range(count)])
+
+
+def gathered(block):
+    along_z = [block] + [swapped(block, "var", 4 * i) for i in (1, 2, 3)]
+    plane = jnp.stack(along_z)
+    across = swapped(plane, "var", 2)
+    return (plane, across, swapped(plane, "var", 1), swapped(across, "var", 1))
+
+
+def added(*terms):
+    total = terms[0].astype(F32)
+    for term in terms[1:]:
+        total = total + term.astype(F32)
+    return total.astype(BF16)
+
+
+def scattered(kept, leaving):
+    plane = added(kept, swapped(leaving, "var", 1))
+    row = added(plane[:4], swapped(plane[4:], "var", 2))
+    mine = added(row[0], *[swapped(row[i], "var", 4 * i) for i in (1, 2, 3)])
+    return (mine, swapped(mine, "win", 1))
+
+
+def prep_kernel(pos_ref, series, target, observed, valid, kept_n, sent_n, kept_t, sent_t, count, total):
+    step = pl.program_id(0)
+    steps = pl.num_programs(0)
+    half = steps // 2
+    local = series.shape[1]
+    rows = series[0]
+    centre = jnp.mean(rows, -1, keepdims=True)
+    offset = rows - centre
+    spread = jnp.sqrt(jnp.mean(offset * offset, -1, keepdims=True) + 1e-05)
+    normed = offset / spread
+    mark = valid[...].astype(F32)
+    weight = observed[0].astype(F32) * mark
+
+    @pl.when(step == 0)
+    def _():
+        total[...] = jnp.zeros_like(total)
+
+    total[...] += jnp.sum(jnp.sum(weight, 0, keepdims=True), 1, keepdims=True)
+    spare = (local, LANES - rows.shape[-1])
+    lane = lane_index(spare)
+    extra_n = jnp.where(lane == 0, mark, 0.0)
+    extra_t = jnp.where(
+        lane == 0,
+        centre,
+        jnp.where(lane == 1, spread, jnp.where(lane == 2, total[0:1, 0:1], 0.0)),
+    )
+    look = rows.shape[-1]
+
+    def write(n_ref, t_ref):
+        n_ref[0, :, 0:look] = normed.astype(BF16)
+        n_ref[0, :, look:LANES] = extra_n.astype(BF16)
+        t_ref[0, :, 0:look] = target[0]
+        t_ref[0, :, look:LANES] = extra_t
+        t_ref[0, :, LANES : LANES + look] = weight
+        t_ref[0, :, LANES + look :] = jnp.zeros(spare, F32)
+
+    @pl.when(step < half)
+    def _():
+        write(kept_n, kept_t)
+
+    @pl.when(step >= half)
+    def _():
+        write(sent_n, sent_t)
+
+    count[...] = total[...]
+
+
+def prep(pos, series, target, observed, valid):
+    windows, local, look = series.shape
+    half = windows // 2
+
+    def source(i, pos_ref):
+        return (lax.rem(pos_ref[0] * half + i, windows), 0, 0)
+
+    def kept(i, pos_ref):
+        return (jnp.minimum(i, half - 1), 0, 0)
+
+    def sent(i, pos_ref):
+        return (jnp.maximum(i - half, 0), 0, 0)
+
+    block = pl.BlockSpec((1, local, look), source)
+    return pl.pallas_call(
+        prep_kernel,
+        grid_spec=pltpu.PrefetchScalarGridSpec(
+            num_scalar_prefetch=1,
+            grid=(windows,),
+            in_specs=[block, block, block, pl.BlockSpec((local, 1), lambda i, p: (0, 0))],
+            out_specs=[
+                pl.BlockSpec((1, local, LANES), kept),
+                pl.BlockSpec((1, local, LANES), sent),
+                pl.BlockSpec((1, local, 2 * LANES), kept),
+                pl.BlockSpec((1, local, 2 * LANES), sent),
+                pl.BlockSpec((8, LANES), lambda i, p: (0, 0)),
+            ],
+            scratch_shapes=[pltpu.VMEM((8, LANES), F32)],
+        ),
+        out_shape=[
+            jax.ShapeDtypeStruct((half, local, LANES), BF16),
+            jax.ShapeDtypeStruct((half, local, LANES), BF16),
+            jax.ShapeDtypeStruct((half, local, 2 * LANES), F32),
+            jax.ShapeDtypeStruct((half, local, 2 * LANES), F32),
+            jax.ShapeDtypeStruct((8, LANES), F32),
+        ],
+        compiler_params=params(),
+        cost_estimate=cost(0, 8 * MIB),
+        name="prep",
+    )(pos, series, target, observed, valid)
+
+
+def pack_first_kernel(joint, embed, out):
+    for c in range(12):
+        out[c * ROWS : (c + 1) * ROWS, :] = joint[0, :, c * LANES : (c + 1) * LANES].astype(BF16)
+    look = embed.shape[-1]
+    out[EMBED_AT:FIRST, 0:look] = embed[...].astype(BF16)
+    out[EMBED_AT:FIRST, look:] = jnp.zeros((ROWS, LANES - look), BF16)
+
+
+def pack_first(joint, embed):
+    return pl.pallas_call(
+        pack_first_kernel,
+        out_shape=jax.ShapeDtypeStruct((FIRST, LANES), BF16),
+        compiler_params=params(),
+        cost_estimate=cost(0, MIB // 2),
+        name="pack_first",
+    )(joint, embed)
+
+
+def pack_second_kernel(own, other, out_w, up, down, head, norm, out):
+    for c in range(4):
+        out[OUT_AT + c * ROWS : OUT_AT + (c + 1) * ROWS, :] = out_w[
+            0, :, c * LANES : (c + 1) * LANES
+        ].astype(BF16)
+    for c in range(16):
+        out[UP_AT + c * ROWS : UP_AT + (c + 1) * ROWS, :] = up[
+            0, :, c * LANES : (c + 1) * LANES
+        ].astype(BF16)
+    for c in range(4):
+        out[DOWN_AT + c * LANES : DOWN_AT + (c + 1) * LANES, :] = down[
+            0, :, c * LANES : (c + 1) * LANES
+        ].astype(BF16)
+    horizon = head.shape[-1]
+    spare = (ROWS, LANES - horizon)
+    lane = lane_index(spare)
+    count = own[0:1, 0:1] + other[...]
+    high = count.astype(BF16).astype(F32)
+    middle = (count - high).astype(BF16).astype(F32)
+    low = (count - high - middle).astype(BF16).astype(F32)
+    extra = jnp.zeros(spare, F32)
+    for i in range(4):
+        extra = jnp.where(lane == i, norm[:, i : i + 1], extra)
+    for i, piece in enumerate((high, middle, low)):
+        extra = jnp.where(lane == 4 + i, piece, extra)
+    out[HEAD_AT:LOSS_AT, 0:horizon] = head[...].astype(BF16)
+    out[HEAD_AT:LOSS_AT, horizon:] = extra.astype(BF16)
+    out[LOSS_AT:BUNDLE, :] = jnp.zeros((BUNDLE - LOSS_AT, LANES), BF16)
+
+
+def pack_second(own, other, out_w, up, down, head, norm):
+    return pl.pallas_call(
+        pack_second_kernel,
+        out_shape=jax.ShapeDtypeStruct((BUNDLE, LANES), BF16),
+        compiler_params=params(),
+        cost_estimate=cost(0, MIB),
+        name="pack_second",
+    )(own, other, out_w, up, down, head, norm)
+
+
+def project_kernel(me_ref, g0, g1, g2, g3, kept, came, qkv, hid, joint, embed):
+    @pl.when(pl.program_id(0) == 0)
+    def _():
+        me = me_ref[0]
+        for slot in range(PARTS):
+            block = (g0, g1, g2, g3)[slot // 4]
+            owner = me ^ offset_of(slot)
+            for c in range(12):
+                joint[owner, :, c * LANES : (c + 1) * LANES] = block[
+                    slot % 4, c * ROWS : (c + 1) * ROWS, :
+                ]
+            embed[owner] = block[slot % 4, EMBED_AT:FIRST, :]
+
+    normed = jnp.concatenate([kept[0], came[0]], axis=0)
+    low = dot_nt(embed[...].reshape(D, LANES), normed).astype(BF16)
+    hid[...] = low
+    for part in range(3):
+        weights = joint[:, :, part * D : (part + 1) * D].reshape(D, D)
+        rows = dot_tn(weights, low)
+        if part == 0:
+            rows = rows.astype(BF16).astype(F32) * 0.125
+        qkv[part * D : (part + 1) * D, :] = rows.astype(BF16)
+
+
+def project(me, bundle, kept, came):
+    half, local, _ = kept.shape
+    slots = 2 * local
+    whole = pl.BlockSpec((4, FIRST, LANES), lambda w, m: (0, 0, 0))
+    mine = pl.BlockSpec((1, local, LANES), lambda w, m: (w, 0, 0))
+    return pl.pallas_call(
+        project_kernel,
+        grid_spec=pltpu.PrefetchScalarGridSpec(
+            num_scalar_prefetch=1,
+            grid=(half,),
+            in_specs=[whole] * 4 + [mine] * 2,
+            out_specs=[
+                pl.BlockSpec((3 * D, slots), lambda w, m: (0, w)),
+                pl.BlockSpec((D, slots), lambda w, m: (0, w)),
+                pl.BlockSpec((PARTS, ROWS, 3 * D), lambda w, m: (0, 0, 0)),
+                pl.BlockSpec((PARTS, ROWS, LANES), lambda w, m: (0, 0, 0)),
+            ],
+        ),
+        out_shape=[
+            jax.ShapeDtypeStruct((3 * D, half * slots), BF16),
+            jax.ShapeDtypeStruct((D, half * slots), BF16),
+            jax.ShapeDtypeStruct((PARTS, ROWS, 3 * D), BF16),
+            jax.ShapeDtypeStruct((PARTS, ROWS, LANES), BF16),
+        ],
+        compiler_params=params(),
+        cost_estimate=cost(3e9, 12 * MIB),
+        name="project",
+    )(me, *bundle, kept, came)
+
+
+def tiles_of(length, size):
+    return [(at, min(size, length - at)) for at in range(0, length, size)]
+
+
+def attend_kernel(kept, came, q, k, v, weights, mixed, scale, bias):
+    slots = q.shape[1]
+    local = slots // 2
+
+    @pl.when((pl.program_id(0) == 0) & (pl.program_id(1) == 0))
+    def _():
+        for part, marks in enumerate((kept, came)):
+            rows = slice(part * local, (part + 1) * local)
+            mark = marks[0, :, 96:97].astype(F32)
+            key = part * local + lax.broadcasted_iota(jnp.int32, (local, slots), 0)
+            query = lane_index((local, slots))
+            bias[rows, :] = jnp.where((mark > 0.5) | (key == query), 0.0, -1e30)
+
+    keys = k[...].T
+    for at, size in tiles_of(slots, 256):
+        cols = slice(at, at + size)
+        score = dot_nn(keys, q[:, cols]) + bias[:, cols]
+        top = jnp.max(score, 0, keepdims=True)
+        weight = jnp.exp(score - top)
+        low = weight.astype(BF16)
+        weights[0, :, cols] = low
+        inverse = 1.0 / jnp.sum(weight, 0, keepdims=True)
+        scale[0, :, cols] = inverse
+        mixed[:, cols] = (dot_nn(v[...], low) * inverse).astype(BF16)
+
+
+def attend(first, count, kept, came, qkv):
+    half, local, _ = kept.shape
+    slots = 2 * local
+    marks = pl.BlockSpec((1, local, LANES), lambda h, w: (0, 0, 0))
+
+    def head(part):
+        return pl.BlockSpec((HEAD_SIZE, slots), lambda h, w: (part * HEADS + first + h, w))
+
+    return pl.pallas_call(
+        attend_kernel,
+        grid=(count, half),
+        in_specs=[marks, marks, head(0), head(1), head(2)],
+        out_specs=[
+            pl.BlockSpec((1, slots, slots), lambda h, w: (h * half + w, 0, 0)),
+            pl.BlockSpec((HEAD_SIZE, slots), lambda h, w: (h, w)),
+            pl.BlockSpec((1, 1, slots), lambda h, w: (h * half + w, 0, 0)),
+        ],
+        out_shape=[
+            jax.ShapeDtypeStruct((count * half, slots, slots), BF16),
+            jax.ShapeDtypeStruct((count * HEAD_SIZE, half * slots), BF16),
+            jax.ShapeDtypeStruct((count * half, 1, slots), F32),
+        ],
+        scratch_shapes=[pltpu.VMEM((slots, slots), F32)],
+        compiler_params=params(),
+        cost_estimate=cost(count * half * 1.2e9, count * half * 2 * MIB),
+        name="attend",
+    )(kept, came, qkv, qkv, qkv)
+
+
+def unattend_kernel(
+    me_ref, weights, scale, mixed, dmixed, q, k, v, hid, dproj, kept, leaving, rows, packed, sems
+):
+    head, window = pl.program_id(0), pl.program_id(1)
+    slots = q.shape[1]
+    dmix = dmixed[...].astype(F32) * scale[0]
+    low = dmix.astype(BF16)
+    delta = jnp.sum(low.astype(F32) * mixed[...].astype(F32), 0, keepdims=True)
+    values = v[...].T
+    keys = k[...]
+    dval = jnp.zeros((HEAD_SIZE, slots), F32)
+    dkey = jnp.zeros((HEAD_SIZE, slots), F32)
+    for at, size in tiles_of(slots, 256):
+        cols = slice(at, at + size)
+        weight = weights[0, :, cols]
+        dweight = dot_nn(values, low[:, cols])
+        dscore = (weight.astype(F32) * (dweight - delta[:, cols])).astype(BF16)
+        dproj[0, :, cols] = (dot_nn(keys, dscore) * 0.125).astype(BF16)
+        dkey = dkey + dot_nt(q[:, cols], dscore)
+        dval = dval + dot_nt(low[:, cols], weight)
+    dproj[1] = dkey.astype(BF16)
+    dproj[2] = dval.astype(BF16)
+    start = pl.multiple_of(window * slots, LANES)
+    for part in range(3):
+        rows[part, head, :, pl.ds(start, slots)] = dproj[part]
+
+    count = pl.num_programs(0)
+
+    @pl.when((head == count - 1) & (window == pl.num_programs(1) - 1))
+    def _():
+        me = me_ref[0]
+        width = rows.shape[1] * HEAD_SIZE
+        for part in range(3):
+            grad = dot_nt(hid[...], rows[part].reshape(width, rows.shape[-1])).astype(BF16)
+            for b in range(PARTS):
+                slot = slot_of(b ^ me)
+                for c in range(width // LANES):
+                    at = (part * (width // LANES) + c) * ROWS
+                    packed[slot, at : at + ROWS, :] = grad[
+                        b * ROWS : (b + 1) * ROWS, c * LANES : (c + 1) * LANES
+                    ]
+        send_packed(packed, kept, leaving, sems)
+
+
+def send_packed(packed, kept, leaving, sems):
+    half = PARTS // 2
+    copies = [
+        pltpu.make_async_copy(packed.at[pl.ds(0, half)], kept, sems.at[0]),
+        pltpu.make_async_copy(packed.at[pl.ds(half, half)], leaving, sems.at[1]),
+    ]
+    for copy in copies:
+        copy.start()
+    for copy in copies:
+        copy.wait()
+
+
+def unattend(me, first, count, weights, scale, mixed, dmixed, qkv, hid):
+    slots = weights.shape[-1]
+    tokens = qkv.shape[1]
+    half = tokens // slots
+    height = 3 * count * HEAD_SIZE // LANES * ROWS
+
+    def head(part):
+        return pl.BlockSpec((HEAD_SIZE, slots), lambda h, w, m: (part * HEADS + first + h, w))
+
+    return pl.pallas_call(
+        unattend_kernel,
+        grid_spec=pltpu.PrefetchScalarGridSpec(
+            num_scalar_prefetch=1,
+            grid=(count, half),
+            in_specs=[
+                pl.BlockSpec((1, slots, slots), lambda h, w, m: (h * half + w, 0, 0)),
+                pl.BlockSpec((1, 1, slots), lambda h, w, m: (h * half + w, 0, 0)),
+                pl.BlockSpec((HEAD_SIZE, slots), lambda h, w, m: (h, w)),
+                pl.BlockSpec((HEAD_SIZE, slots), lambda h, w, m: (first + h, w)),
+                head(0),
+                head(1),
+                head(2),
+                pl.BlockSpec((D, tokens), lambda h, w, m: (0, 0)),
+            ],
+            out_specs=[
+                pl.BlockSpec((3, HEAD_SIZE, slots), lambda h, w, m: (0, h, w)),
+                pl.BlockSpec(memory_space=pl.ANY),
+                pl.BlockSpec(memory_space=pl.ANY),
+            ],
+            scratch_shapes=[
+                pltpu.VMEM((3, count, HEAD_SIZE, tokens), BF16),
+                pltpu.VMEM((PARTS, height, LANES), BF16),
+                pltpu.SemaphoreType.DMA((2,)),
+            ],
+        ),
+        out_shape=[
+            jax.ShapeDtypeStruct((3, count * HEAD_SIZE, tokens), BF16),
+            jax.ShapeDtypeStruct((PARTS // 2, height, LANES), BF16),
+            jax.ShapeDtypeStruct((PARTS // 2, height, LANES), BF16),
+        ],
+        compiler_params=params(),
+        cost_estimate=cost(count * half * 2.5e9, count * half * 2 * MIB),
+        name="unattend",
+    )(me, weights, scale, mixed, dmixed, qkv, qkv, qkv, hid)
+
+
+def gelu_parts(pre):
+    bell = jnp.exp(pre * pre * -0.5)
+    size = jnp.abs(pre)
+    t = 1.0 / (1.0 + 0.23164190 * size)
+    poly = t * (
+        0.127414796
+        + t * (-0.142248368 + t * (0.7107068705 + t * (-0.7265760135 + t * 0.5307027145)))
+    )
+    tail = poly * bell
+    phi = jnp.where(pre >= 0.0, 1.0 - tail, tail)
+    return (pre * phi, phi + pre * bell * 0.3989422804014327)
+
+
+def norm_forward(resid, gain, shift):
+    centre = jnp.mean(resid, 0, keepdims=True)
     offset = resid - centre
-    spread = jnp.mean(offset * offset, -1, keepdims=True)
-    return offset * lax.rsqrt(spread + 1e-05) * gain + shift
+    inverse = lax.rsqrt(jnp.mean(offset * offset, 0, keepdims=True) + 1e-05)
+    unit = offset * inverse
+    return (unit * gain + shift, unit, inverse)
+
+
+def norm_backward(grad, unit, inverse, gain):
+    scaled = grad * gain
+    first = jnp.mean(scaled, 0, keepdims=True)
+    second = jnp.mean(scaled * unit, 0, keepdims=True)
+    return (scaled - first - unit * second) * inverse
+
+
+def middle_kernel(
+    me_ref,
+    g0,
+    g1,
+    g2,
+    g3,
+    embed,
+    normed,
+    future,
+    mixed_a,
+    mixed_b,
+    dmixed,
+    dattn,
+    counted,
+    kept,
+    leaving,
+    w_out,
+    w_up,
+    w_down,
+    w_head,
+    t_out,
+    t_up,
+    t_down,
+    norms,
+    slope,
+    mixed_s,
+    middle_s,
+    active_s,
+    dbranch_s,
+    dpre_s,
+    dattn_s,
+    final_s,
+    dguess_s,
+    norm_sums,
+    loss_sum,
+    packed,
+    sems,
+):
+    step = pl.program_id(0)
+    size = dmixed.shape[1]
+    ff = active_s.shape[0]
+    chunks = ff // D
+
+    @pl.when(step == 0)
+    def _():
+        me = me_ref[0]
+        total = jnp.zeros((1, 1), F32)
+        for slot in range(PARTS):
+            block = (g0, g1, g2, g3)[slot // 4]
+            i = slot % 4
+            owner = me ^ offset_of(slot)
+            for c in range(4):
+                cols = slice(c * LANES, (c + 1) * LANES)
+                at = OUT_AT + c * ROWS
+                w_out[owner, :, cols] = block[i, at : at + ROWS, :]
+                at = DOWN_AT + c * LANES
+                w_down[owner, :, cols] = block[i, at : at + LANES, :]
+            for c in range(16):
+                at = UP_AT + c * ROWS
+                w_up[owner, :, c * LANES : (c + 1) * LANES] = block[i, at : at + ROWS, :]
+            head = block[i, HEAD_AT:LOSS_AT, :]
+            w_head[owner] = head
+            pieces = head[0:1, 100:103].astype(F32)
+            total = total + jnp.sum(pieces, 1, keepdims=True)
+        counted[...] = jnp.broadcast_to(jnp.maximum(total, 1.0), counted.shape)
+        t_out[...] = w_out[...].reshape(D, D).T
+        for c in range(chunks):
+            rows = slice(c * D, (c + 1) * D)
+            t_up[rows, :] = w_up[:, :, rows].reshape(D, D).T
+            t_down[:, rows] = w_down[c * 4 : (c + 1) * 4].reshape(D, D).T
+        extra = w_head[...].reshape(D, LANES)
+        for i in range(4):
+            column = extra[:, 96 + i : 97 + i].astype(F32)
+            norms[i] = jnp.broadcast_to(column, (D, size))
+        norm_sums[...] = jnp.zeros_like(norm_sums)
+        loss_sum[...] = jnp.zeros_like(loss_sum)
+
+    cols = pl.ds(pl.multiple_of(step * size, size), size)
+    unit_of = normed[...]
+    mixed = jnp.concatenate([mixed_a[...], mixed_b[...]], axis=0)
+    mixed_s[:, cols] = mixed
+    resid = dot_nt(embed[...].reshape(D, LANES), unit_of) + dot_nn(t_out[...], mixed)
+    middle, unit_one, inverse_one = norm_forward(resid, norms[0], norms[1])
+    middle_low = middle.astype(BF16)
+    middle_s[:, cols] = middle_low
+    resid = middle
+    for c in range(chunks):
+        rows = slice(c * D, (c + 1) * D)
+        active, gradient = gelu_parts(dot_nn(t_up[rows, :], middle_low))
+        active = active.astype(BF16)
+        active_s[rows, cols] = active
+        slope[rows, :] = gradient
+        resid = resid + dot_nn(t_down[:, rows], active)
+    final, unit_two, inverse_two = norm_forward(resid, norms[2], norms[3])
+    final_low = final.astype(BF16)
+    final_s[:, cols] = final_low
+    w_h = w_head[...].reshape(D, LANES)
+    guess = dot_tn(final_low, w_h)
+    ahead = future[:, 0:LANES]
+    weighting = future[:, LANES:]
+    centre = future[:, 96:97]
+    spread = future[:, 97:98]
+    error = guess * spread + centre - ahead
+    loss_sum[...] += jnp.sum(weighting * error * error, 0, keepdims=True)
+    dguess = (2.0 * weighting * error / counted[0:1, 0:1] * spread).astype(BF16)
+    dguess_s[cols, :] = dguess
+    dfinal = dot_nt(w_h, dguess)
+    norm_sums[2] += dfinal * unit_two
+    norm_sums[3] += dfinal
+    dresid = norm_backward(dfinal, unit_two, inverse_two, norms[2])
+    dbranch = dresid.astype(BF16)
+    dbranch_s[:, cols] = dbranch
+    for c in range(chunks):
+        rows = slice(c * D, (c + 1) * D)
+        w_d = w_down[c * 4 : (c + 1) * 4].reshape(D, D)
+        dpre = (dot_nn(w_d, dbranch) * slope[rows, :]).astype(BF16)
+        dpre_s[rows, cols] = dpre
+        dresid = dresid + dot_nn(w_up[:, :, rows].reshape(D, D), dpre)
+    norm_sums[0] += dresid * unit_one
+    norm_sums[1] += dresid
+    dfirst = norm_backward(dresid, unit_one, inverse_one, norms[0]).astype(BF16)
+    dattn[...] = dfirst
+    dattn_s[:, cols] = dfirst
+    dmixed[...] = dot_nn(w_out[...].reshape(D, D), dfirst).astype(BF16)
+
+    @pl.when(step == pl.num_programs(0) - 1)
+    def _():
+        me = me_ref[0]
+
+        def place(grad, first_row, blocks, base):
+            height = grad.shape[0] // blocks
+            for b in range(blocks):
+                slot = slot_of((first_row + b) ^ me)
+                for c in range(grad.shape[1] // LANES):
+                    at = base + c * height
+                    packed[slot, at : at + height, :] = grad[
+                        b * height : (b + 1) * height, c * LANES : (c + 1) * LANES
+                    ]
+
+        for c in range(chunks):
+            rows = slice(c * D, (c + 1) * D)
+            place(dot_nt(active_s[rows, :], dbranch_s[...]).astype(BF16), c * 4, 4, DOWN_AT)
+            place(
+                dot_nt(middle_s[...], dpre_s[rows, :]).astype(BF16),
+                0,
+                PARTS,
+                UP_AT + c * (D // LANES) * ROWS,
+            )
+        place(dot_nt(mixed_s[...], dattn_s[...]).astype(BF16), 0, PARTS, OUT_AT)
+        head = dot_nn(final_s[...], dguess_s[...])
+        lane = lane_index(head.shape)
+        for i in range(4):
+            head = jnp.where(lane == 96 + i, jnp.sum(norm_sums[i], 1, keepdims=True), head)
+        place(head.astype(BF16), 0, PARTS, HEAD_AT)
+        row = lax.broadcasted_iota(jnp.int32, (BUNDLE - LOSS_AT, LANES), 0)
+        losses = jnp.where(row == 0, loss_sum[...], 0.0).astype(BF16)
+        for slot in range(PARTS):
+            packed[slot, LOSS_AT:BUNDLE, :] = losses
+        send_packed(packed, kept, leaving, sems)
+
+
+def middle_pass(me, bundle, embed, normed, future, mixed, ff):
+    tokens = normed.shape[0]
+    size = 256
+    whole = pl.BlockSpec((4, BUNDLE, LANES), lambda t, m: (0, 0, 0), pipeline_mode=pl.Buffered(1))
+    return pl.pallas_call(
+        middle_kernel,
+        grid_spec=pltpu.PrefetchScalarGridSpec(
+            num_scalar_prefetch=1,
+            grid=(tokens // size,),
+            in_specs=[whole] * 4
+            + [
+                pl.BlockSpec((PARTS, ROWS, LANES), lambda t, m: (0, 0, 0)),
+                pl.BlockSpec((size, LANES), lambda t, m: (t, 0)),
+                pl.BlockSpec((size, 2 * LANES), lambda t, m: (t, 0)),
+                pl.BlockSpec((D // 2, size), lambda t, m: (0, t)),
+                pl.BlockSpec((D // 2, size), lambda t, m: (0, t)),
+            ],
+            out_specs=[
+                pl.BlockSpec((D, size), lambda t, m: (0, t)),
+                pl.BlockSpec((D, size), lambda t, m: (0, t)),
+                pl.BlockSpec((8, LANES), lambda t, m: (0, 0)),
+                pl.BlockSpec(memory_space=pl.ANY),
+                pl.BlockSpec(memory_space=pl.ANY),
+            ],
+            scratch_shapes=[
+                pltpu.VMEM((PARTS, ROWS, D), BF16),
+                pltpu.VMEM((PARTS, ROWS, ff), BF16),
+                pltpu.VMEM((PARTS, ff // PARTS, D), BF16),
+                pltpu.VMEM((PARTS, ROWS, LANES), BF16),
+                pltpu.VMEM((D, D), BF16),
+                pltpu.VMEM((ff, D), BF16),
+                pltpu.VMEM((D, ff), BF16),
+                pltpu.VMEM((4, D, size), F32),
+                pltpu.VMEM((ff, size), F32),
+                pltpu.VMEM((D, tokens), BF16),
+                pltpu.VMEM((D, tokens), BF16),
+                pltpu.VMEM((ff, tokens), BF16),
+                pltpu.VMEM((D, tokens), BF16),
+                pltpu.VMEM((ff, tokens), BF16),
+                pltpu.VMEM((D, tokens), BF16),
+                pltpu.VMEM((D, tokens), BF16),
+                pltpu.VMEM((tokens, LANES), BF16),
+                pltpu.VMEM((4, D, size), F32),
+                pltpu.VMEM((1, LANES), F32),
+                pltpu.VMEM((PARTS, BUNDLE, LANES), BF16),
+                pltpu.SemaphoreType.DMA((2,)),
+            ],
+        ),
+        out_shape=[
+            jax.ShapeDtypeStruct((D, tokens), BF16),
+            jax.ShapeDtypeStruct((D, tokens), BF16),
+            jax.ShapeDtypeStruct((8, LANES), F32),
+            jax.ShapeDtypeStruct((PARTS // 2, BUNDLE, LANES), BF16),
+            jax.ShapeDtypeStruct((PARTS // 2, BUNDLE, LANES), BF16),
+        ],
+        compiler_params=params(60),
+        cost_estimate=cost(35e9, 20 * MIB),
+        name="middle",
+    )(me, *bundle, embed, normed, future, *mixed)
+
+
+def last_kernel(me_ref, joint, dproj_a, dproj_b, dattn, normed, kept, leaving, total, packed, sems):
+    step = pl.program_id(0)
+
+    @pl.when(step == 0)
+    def _():
+        total[...] = jnp.zeros_like(total)
+
+    dhidden = dattn[...].astype(F32)
+    for part in range(3):
+        rows = jnp.concatenate([dproj_a[part], dproj_b[part]], axis=0)
+        weights = joint[:, :, part * D : (part + 1) * D].reshape(D, D)
+        dhidden = dhidden + dot_nn(weights, rows)
+    total[...] += dot_nn(dhidden.astype(BF16), normed[...])
+
+    @pl.when(step == pl.num_programs(0) - 1)
+    def _():
+        me = me_ref[0]
+        for b in range(PARTS):
+            packed[slot_of(b ^ me)] = total[b * ROWS : (b + 1) * ROWS, :].astype(BF16)
+        send_packed(packed, kept, leaving, sems)
+
+
+def last_pass(me, joint, dprojs, dattn, normed):
+    tokens = normed.shape[0]
+    size = 256
+    return pl.pallas_call(
+        last_kernel,
+        grid_spec=pltpu.PrefetchScalarGridSpec(
+            num_scalar_prefetch=1,
+            grid=(tokens // size,),
+            in_specs=[
+                pl.BlockSpec((PARTS, ROWS, 3 * D), lambda t, m: (0, 0, 0)),
+                pl.BlockSpec((3, D // 2, size), lambda t, m: (0, 0, t)),
+                pl.BlockSpec((3, D // 2, size), lambda t, m: (0, 0, t)),
+                pl.BlockSpec((D, size), lambda t, m: (0, t)),
+                pl.BlockSpec((size, LANES), lambda t, m: (t, 0)),
+            ],
+            out_specs=[pl.BlockSpec(memory_space=pl.ANY), pl.BlockSpec(memory_space=pl.ANY)],
+            scratch_shapes=[
+                pltpu.VMEM((D, LANES), F32),
+                pltpu.VMEM((PARTS, ROWS, LANES), BF16),
+                pltpu.SemaphoreType.DMA((2,)),
+            ],
+        ),
+        out_shape=[
+            jax.ShapeDtypeStruct((PARTS // 2, ROWS, LANES), BF16),
+            jax.ShapeDtypeStruct((PARTS // 2, ROWS, LANES), BF16),
+        ],
+        compiler_params=params(),
+        cost_estimate=cost(3e9, 10 * MIB),
+        name="last",
+    )(me, joint, *dprojs, dattn, normed)
 
 
 def adamw(weight, mean, square, grad, count_step):
@@ -31,6 +755,207 @@
     square_hat = square_next / (1.0 - 0.999**count_step)
     weight_next = weight - 0.1 * (mean_hat / (jnp.sqrt(square_hat) + 1e-08) + 0.1 * weight)
     return (weight_next, mean_next, square_next)
+
+
+def step_second_kernel(mine, other, counted, *refs):
+    held, results = refs[:15], refs[15:]
+    grad = mine[...].astype(F32) + other[...].astype(F32)
+
+    def update(which, at, value):
+        states = [held[which * 3 + j] for j in range(3)]
+        news = adamw(*[state[at] for state in states], value, float(STEP_NUMBER))
+        for j in range(3):
+            results[which * 3 + j][at] = news[j]
+
+    def block(c):
+        return slice(c * LANES, (c + 1) * LANES)
+
+    for c in range(4):
+        base = OUT_AT + c * ROWS
+        update(0, (0, slice(None), block(c)), grad[base : base + ROWS])
+    for c in range(16):
+        base = UP_AT + c * ROWS
+        update(1, (0, slice(None), block(c)), grad[base : base + ROWS])
+    for c in range(4):
+        base = DOWN_AT + c * LANES
+        update(2, (0, slice(None), block(c)), grad[base : base + LANES])
+    horizon = held[9].shape[-1]
+    head = grad[HEAD_AT:LOSS_AT]
+    update(3, (slice(None), slice(None)), head[:, 0:horizon])
+    norm = head[:, 96:100]
+    update(4, (slice(None), slice(None)), norm)
+    results[15][...] = norm
+    losses = jnp.sum(grad[LOSS_AT : LOSS_AT + 1], 1, keepdims=True)
+    results[16][...] = losses / counted[0:1, 0:1]
+
+
+def step_second(mine, other, counted, states):
+    shapes = [jax.ShapeDtypeStruct(a.shape, F32) for a in states]
+    return pl.pallas_call(
+        step_second_kernel,
+        out_shape=shapes
+        + [jax.ShapeDtypeStruct(states[12].shape, F32), jax.ShapeDtypeStruct((1, 1), F32)],
+        compiler_params=params(),
+        cost_estimate=cost(0, 5 * MIB),
+        name="step_second",
+    )(mine, other, counted, *states)
+
+
+def step_first_kernel(mine_a, other_a, mine_b, other_b, *refs):
+    held, results = refs[:6], refs[6:]
+    halves = [
+        mine_a[...].astype(F32) + other_a[...].astype(F32),
+        mine_b[...].astype(F32) + other_b[...].astype(F32),
+    ]
+
+    def update(which, at, value):
+        states = [held[which * 3 + j] for j in range(3)]
+        news = adamw(*[state[at] for state in states], value, float(STEP_NUMBER))
+        for j in range(3):
+            results[which * 3 + j][at] = news[j]
+
+    for part in range(3):
+        for side in range(2):
+            for c in range(2):
+                at = (part * 2 + c) * ROWS
+                start = part * D + side * (D // 2) + c * LANES
+                update(0, (0, slice(None), slice(start, start + LANES)), halves[side][at : at + ROWS])
+    look = held[3].shape[-1]
+    update(1, (slice(None), slice(None)), halves[1][6 * ROWS : 7 * ROWS, 0:look])
+
+
+def step_first(pair_a, pair_b, states):
+    shapes = [jax.ShapeDtypeStruct(a.shape, F32) for a in states]
+    return pl.pallas_call(
+        step_first_kernel,
+        out_shape=shapes,
+        compiler_params=params(),
+        cost_estimate=cost(0, 2 * MIB),
+        name="step_first",
+    )(*pair_a, *pair_b, *states)
+
+
+def whole_windows_body(
+    series,
+    target,
+    valid_slots,
+    observed,
+    embed_weight,
+    joint_proj,
+    out_proj,
+    up_proj,
+    down_proj,
+    head_weight,
+    norm_params,
+    embed_mean,
+    joint_mean,
+    out_mean,
+    up_mean,
+    down_mean,
+    head_mean,
+    norm_mean,
+    embed_square,
+    joint_square,
+    out_square,
+    up_square,
+    down_square,
+    head_square,
+    norm_square,
+):
+    me = lax.axis_index("var").astype(jnp.int32).reshape(1)
+    pos = lax.axis_index("win").astype(jnp.int32).reshape(1)
+    ff = up_proj.shape[-1]
+    first = gathered(pack_first(joint_proj, embed_weight.T))
+    valid = valid_slots.reshape(-1, 1)
+    kept_n, sent_n, kept_t, sent_t, own = prep(pos, series, target, observed, valid)
+    came_n = swapped(sent_n, "win", 1)
+    came_t = swapped(sent_t, "win", 1)
+    half, local, _ = kept_n.shape
+    tokens = half * 2 * local
+    second = gathered(
+        pack_second(
+            own,
+            came_t[half - 1, 0:1, 98:99],
+            out_proj,
+            up_proj,
+            down_proj,
+            head_weight,
+            norm_params[0].T,
+        )
+    )
+    normed = jnp.concatenate([kept_n, came_n], axis=1).reshape(tokens, LANES)
+    future = jnp.concatenate([kept_t, came_t], axis=1).reshape(tokens, 2 * LANES)
+    qkv, hid, joint, embed = project(me, first, kept_n, came_n)
+    count = HEADS // 2
+    sides = [attend(side * count, count, kept_n, came_n, qkv) for side in range(2)]
+    dmixed, dattn, counted, kept, leaving = middle_pass(
+        me, second, embed, normed, future, [side[1] for side in sides], ff
+    )
+    second_pair = scattered(kept, leaving)
+    grads = [
+        unattend(me, side * count, count, sides[side][0], sides[side][2], sides[side][1], dmixed, qkv, hid)
+        for side in range(2)
+    ]
+    pair_a = scattered(grads[0][1], grads[0][2])
+    last = last_pass(me, joint, [g[0] for g in grads], dattn, normed)
+    pair_b = scattered(
+        *[jnp.concatenate([grads[1][1 + i], last[i]], axis=1) for i in range(2)]
+    )
+    states = []
+    for group in (
+        (out_proj, out_mean, out_square),
+        (up_proj, up_mean, up_square),
+        (down_proj, down_mean, down_square),
+        (head_weight, head_mean, head_square),
+        (norm_params[0].T, norm_mean[0].T, norm_square[0].T),
+    ):
+        states.extend(group)
+    new = step_second(*second_pair, counted, states)
+    fresh = step_first(
+        pair_a,
+        pair_b,
+        [joint_proj, joint_mean, joint_square, embed_weight.T, embed_mean.T, embed_square.T],
+    )
+    outs, ups, downs, heads, norms = [new[3 * i : 3 * i + 3] for i in range(5)]
+    norms = [n.T[None] for n in norms]
+    embeds = [e.T for e in fresh[3:6]]
+    return (
+        new[16].reshape(1),
+        embeds[0],
+        fresh[0],
+        outs[0],
+        ups[0],
+        downs[0],
+        heads[0],
+        new[15].T[None],
+        embeds[1],
+        fresh[1],
+        outs[1],
+        ups[1],
+        downs[1],
+        heads[1],
+        norms[1],
+        embeds[2],
+        fresh[2],
+        outs[2],
+        ups[2],
+        downs[2],
+        heads[2],
+        norms[2],
+    )
+
+
+def passed_along(block, axis, distance):
+    devices = range(lax.axis_size(axis))
+    route = [((i - distance) % len(devices), i) for i in devices]
+    return lax.ppermute(block, axis, route)
+
+
+def layer_norm(resid, gain, shift):
+    centre = jnp.mean(resid, -1, keepdims=True)
+    offset = resid - centre
+    spread = jnp.mean(offset * offset, -1, keepdims=True)
+    return offset * lax.rsqrt(spread + 1e-05) * gain + shift
 
 
 def to_items(matrix, windows, local, parts):
@@ -251,7 +1176,7 @@
     return (dhidden, (grad_joint, grad_out, grad_up, grad_down, grad_norm))
 
 
-def body(
+def sliced_windows_body(
     series,
     target,
     valid_slots,
@@ -399,6 +1324,8 @@
 
 
 def solution(mesh):
+    swaps = mesh.shape["var"] == PARTS and mesh.shape["win"] == 2
+    body = whole_windows_body if swaps else sliced_windows_body
     placed = (
         P("var", "win", None),
         P("var", "win", None),

time: 1430 us -> 385 us (0.27)
  waiting for transfers between devices: 647 us -> 121 us
  matrix products: 342 us -> 0 us
  Pallas kernels: 0 us -> 190 us
  local copies, waits for them, and re-layouts: 177 us -> 15.2 us
  blocking collectives: 133 us -> 0 us
  other arithmetic: 95.2 us -> 6.08 us
  starting transfers between devices: 10.8 us -> 50.9 us
  between operations: 17.8 us -> 1.05 us
    dot_general x30 -> x0, matrix products: 342 us -> none  [the longest x4 59.1 us: masked_scores(): jnp.einsum('acn,azn->acz', query_rows, key_portion, preferred_element_typ...]
    reduce_scatter x6 -> x0, waiting for transfers between devices: 323 us -> none  [the longest x1 64.7 us: body(): lax.psum_scatter(stacked[2].astype(jnp.bfloat16), 'var', scatter_dimensio...]
    pallas_call x0 -> x12, Pallas kernels: none -> 190 us  [the longest x1 59.6 us: middle_pass(): pl.pallas_call(middle_kernel, grid_spec=pltpu.PrefetchScalarGridSpec(num_...]
    ppermute x8 -> x32, waiting for transfers between devices: 286 us -> 121 us  [swapped(): return lax.ppermute(block, axis, [(i, i ^ distance) for i in range(count)])]
    all_gather x4 -> x0, blocking collectives: 84.5 us -> none  [the longest x1 23.6 us: body(): lax.all_gather(embed_weight.astype(jnp.bfloat16), 'var', axis=1, tiled=True)]
    psum x2 -> x0, blocking collectives: 48.5 us -> none  [the longest x1 39.2 us: body(): loss = lax.psum(loss_part, ('var', 'win')) / count]
    while x21 -> x0, local copies, waits for them, and re-layouts: 44.6 us -> none
    reshape x7 -> x1, local copies, waits for them, and re-layouts: 42.9 us -> 0.84 us  [whole_windows_body(): valid = valid_slots.reshape(-1, 1)]
  transfers between devices with their start and end apart: 19 -> 32, of which waited for: 13 -> 11; matrix products, arithmetic and copies ran while one was open for 23% -> 2% of each run, Pallas kernels for 0% -> 31%
where the time goes in v1:
time: 385 us; the launch traced here: 384 us
  Pallas kernels  190 us (49%)
  waiting for transfers between devices  121 us (31%)
  starting transfers between devices  50.9 us (13%)
  local copies, waits for them, and re-layouts  15.2 us (4%)
  other arithmetic  6.08 us (2%)
    ppermute x32, waiting for transfers between devices, swapped(): return lax.ppermute(block, axis, [(i, i ^ distance) for i in range(count)])  121 us
    pallas_call x1, Pallas kernels, middle_pass(): pl.pallas_call(middle_kernel, grid_spec=pltpu.PrefetchScalarGridSpec(num_...  59.6 us
    pallas_call x2, Pallas kernels, unattend(): pl.pallas_call(unattend_kernel, grid_spec=pltpu.PrefetchScalarGridSpec(nu...  51.3 us
    ppermute x32, starting transfers between devices, swapped(): return lax.ppermute(block, axis, [(i, i ^ distance) for i in range(count)])  50.9 us
    pallas_call x2, Pallas kernels, attend(): pl.pallas_call(attend_kernel, grid=(count, half), in_specs=[marks, marks,...  46 us
    pallas_call x1, Pallas kernels, last_pass(): pl.pallas_call(last_kernel, grid_spec=pltpu.PrefetchScalarGridSpec(num_sc...  9.63 us
  transfers between devices with their start and end apart: 32, of which 11 were waited for; matrix products, arithmetic and copies ran while one was open for 2% of the time, Pallas kernels for 31%

profile of v1, /device:TPU:0, one launch (start us, length us, event | category | flops | bytes accessed | tf_op | source)
XLA Modules:
  0.0 383.9 jit_solution(3317619678768090774)
XLA Ops:
  0.7 2.5 copy.56.series
  3.2 1.3 copy.57.target
  4.5 1.3 copy.58.observed
  5.7 0.8 copy.59.valid
  6.6 6.0 %prep.1 = (bf16[2,448,128]{2,1,0:T(8,128)(2,1)}, bf16[2,448,128]{2,1,0:T(8,128)(2,1)}, f32[2,448,256]{2,1,0:T(8,128)}, f32[2,448,256]{2,1,0:T(8,128)}, f32[8,128]{1,0:T(8,128)}) custom-call(s32[1]{0:T(128)} %bitcast.1.pos_ref, f32[4,448,96]{2,1,0:T(8,128)} %copy.56.series, f32[4,448,96]{2,1,0:T(8,128)} %copy.57.target, s32[4,448,96]{2,1,0:T(8,128)} %copy.58.observed, ...), custom_call_target="tpu_custom_call" | custom-call | bytes 8388608 | tf_op jit(solution)/shard_map/prep/pallas_call | solution.py:146
  12.6 3.0 collective-permute-start
  15.6 0.7 copy.60
  16.3 19.9 %collective-permute-done = f32[2,448,256]{2,1,0:T(8,128)S(1)} collective-permute-done((f32[2,448,256]{2,1,0:T(8,128)}, f32[2,448,256]{2,1,0:T(8,128)S(1)}, u32[]{:S(2)}, u32[]{:S(2)}) %collective-permute-start) | collective-permute-done | bytes 917536 | tf_op jit(solution)/shard_map/ppermute | solution.py:61
  36.1 0.6 slice.76
  36.7 2.6 pack_second.1
  39.3 1.8 collective-permute-start.1
  41.1 2.6 collective-permute-start.2
  43.7 1.6 pack_first.1
  45.3 0.9 collective-permute-start.7
  46.2 3.5 collective-permute-start.8
  49.7 4.8 %collective-permute-done.1 = bf16[1200,128]{1,0:T(8,128)(2,1)S(1)} collective-permute-done((bf16[1200,128]{1,0:T(8,128)(2,1)}, bf16[1200,128]{1,0:T(8,128)(2,1)S(1)}, u32[]{:S(2)}, u32[]{:S(2)}) %collective-permute-start.1) | collective-permute-done | bytes 307232 | tf_op jit(solution)/shard_map/ppermute | solution.py:61
  54.5 4.5 %collective-permute-start.9 = (bf16[416,128]{1,0:T(8,128)(2,1)}, bf16[416,128]{1,0:T(8,128)(2,1)S(1)}, u32[]{:S(2)}, u32[]{:S(2)}) collective-permute-start(bf16[416,128]{1,0:T(8,128)(2,1)} %pack_first.1), channel_id=1, source_target_pairs={{0,24},{2,26},{4,28},{6,30},{8,16},{10,18},{12,20},{14,22},{16,8},... | collective-permute-start | bytes 319496 | tf_op jit(solution)/shard_map/ppermute | solution.py:61
  59.0 11.2 %collective-permute-done.2 = bf16[1200,128]{1,0:T(8,128)(2,1)S(1)} collective-permute-done((bf16[1200,128]{1,0:T(8,128)(2,1)}, bf16[1200,128]{1,0:T(8,128)(2,1)S(1)}, u32[]{:S(2)}, u32[]{:S(2)}) %collective-permute-start.2) | collective-permute-done | bytes 307232 | tf_op jit(solution)/shard_map/ppermute | solution.py:61
  70.2 1.2 pad_maximum_fusion.1.g0
  71.4 1.6 collective-permute-start.4
  73.0 4.9 %collective-permute-done.8 = bf16[416,128]{1,0:T(8,128)(2,1)S(1)} collective-permute-done((bf16[416,128]{1,0:T(8,128)(2,1)}, bf16[416,128]{1,0:T(8,128)(2,1)S(1)}, u32[]{:S(2)}, u32[]{:S(2)}) %collective-permute-start.8) | collective-permute-done | bytes 106528 | tf_op jit(solution)/shard_map/ppermute | solution.py:61
  78.0 1.6 collective-permute-start.10
  79.6 1.5 collective-permute-start.13
  81.1 19.6 %collective-permute-done.10.g1 = bf16[4,416,128]{2,1,0:T(8,128)(2,1)} collective-permute-done((bf16[4,416,128]{2,1,0:T(8,128)(2,1)S(1)}, bf16[4,416,128]{2,1,0:T(8,128)(2,1)}, u32[]{:S(2)}, u32[]{:S(2)}) %collective-permute-start.10) | collective-permute-done | bytes 426016 | tf_op jit(solution)/shard_map/ppermute | solution.py:61
  100.6 1.9 pad_maximum_fusion.2
  102.5 1.3 pad_maximum_fusion
  103.9 7.6 %project.1 = (bf16[1536,1792]{1,0:T(8,128)(2,1)}, bf16[512,1792]{1,0:T(8,128)(2,1)}, bf16[16,32,1536]{2,1,0:T(8,128)(2,1)}, bf16[16,32,128]{2,1,0:T(8,128)(2,1)}) custom-call(s32[1]{0:T(128)} %bitcast.me_ref, bf16[4,416,128]{2,1,0:T(8,128)(2,1)} %copy-done.7, bf16[4,416,128]{2,1,0:T(8,128)(2,1)} %collective-permute-done.10.g1, ...), custom_call_target="tpu_custom_call" | custom-call | flops 3000000000 | bytes 12582912 | tf_op jit(solution)/shard_map/project/pallas_call | solution.py:261
  111.4 0.6 collective-permute-start.5
  112.1 23.0 %attend.3 = (bf16[8,896,896]{2,1,0:T(8,128)(2,1)}, bf16[256,1792]{1,0:T(8,128)(2,1)}, f32[8,1,896]{2,1,0:T(1,128)}) custom-call(bf16[2,448,128]{2,1,0:T(8,128)(2,1)} %get-tuple-element.74.kept, bf16[2,448,128]{2,1,0:T(8,128)(2,1)} %collective-permute-done.13.came, bf16[1536,1792]{1,0:T(8,128)(2,1)} %get-tuple-element.78.q.k.v, ...), custom_call_target="tpu_custom_call" | custom-call | flops 9600000000 | bytes 16777216 | tf_op jit(solution)/shard_map/attend/pallas_call | solution.py:324
  135.1 22.9 %attend.2 = (bf16[8,896,896]{2,1,0:T(8,128)(2,1)}, bf16[256,1792]{1,0:T(8,128)(2,1)}, f32[8,1,896]{2,1,0:T(1,128)}) custom-call(bf16[2,448,128]{2,1,0:T(8,128)(2,1)} %get-tuple-element.74.kept, bf16[2,448,128]{2,1,0:T(8,128)(2,1)} %collective-permute-done.13.came, bf16[1536,1792]{1,0:T(8,128)(2,1)} %get-tuple-element.78.q.k.v, ...), custom_call_target="tpu_custom_call" | custom-call | flops 9600000000 | bytes 16777216 | tf_op jit(solution)/shard_map/attend/pallas_call | solution.py:324
  158.1 1.0 copy-done.22
  159.1 59.6 %middle.1 = (bf16[512,1792]{1,0:T(8,128)(2,1)}, bf16[512,1792]{1,0:T(8,128)(2,1)}, f32[8,128]{1,0:T(8,128)}, bf16[8,1200,128]{2,1,0:T(8,128)(2,1)}, bf16[8,1200,128]{2,1,0:T(8,128)(2,1)}) custom-call(s32[1]{0:T(128)} %bitcast.me_ref, bf16[4,1200,128]{2,1,0:T(8,128)(2,1)} %copy-done.1, bf16[4,1200,128]{2,1,0:T(8,128)(2,1)} %collective-permute-done.4.g1, ...), custom_call_target="tpu_custom_call" | custom-call | flops 35000000512 | bytes 20971520 | tf_op jit(solution)/shard_map/middle/pallas_call | solution.py:640
  218.7 0.5 collective-permute-start.14
  219.2 25.6 %unattend.2 = (bf16[3,256,1792]{2,1,0:T(8,128)(2,1)}, bf16[8,192,128]{2,1,0:T(8,128)(2,1)}, bf16[8,192,128]{2,1,0:T(8,128)(2,1)}) custom-call(s32[1]{0:T(128)} %bitcast.me_ref, bf16[8,896,896]{2,1,0:T(8,128)(2,1)} %get-tuple-element.85.weights, f32[8,1,896]{2,1,0:T(1,128)} %get-tuple-element.86.scale, bf16[256,1792]{1,0:T(8,128)(2,1)} %get-tuple-element.79.mixed_a.mixed, ...), custom_call_target="tpu_custom_call" | custom-call | flops 20000000000 | bytes 16777216 | tf_op jit(solution)/shard_map/unattend/pallas_call | solution.py:410
  245.0 25.7 %unattend.3 = (bf16[3,256,1792]{2,1,0:T(8,128)(2,1)}, bf16[8,192,128]{2,1,0:T(8,128)(2,1)}, bf16[8,192,128]{2,1,0:T(8,128)(2,1)}) custom-call(s32[1]{0:T(128)} %bitcast.me_ref, bf16[8,896,896]{2,1,0:T(8,128)(2,1)} %get-tuple-element.91.weights, f32[8,1,896]{2,1,0:T(1,128)} %get-tuple-element.92.scale, bf16[256,1792]{1,0:T(8,128)(2,1)} %get-tuple-element.80.mixed_b.mixed, ...), custom_call_target="tpu_custom_call" | custom-call | flops 20000000000 | bytes 16777216 | tf_op jit(solution)/shard_map/unattend/pallas_call | solution.py:410
  270.7 9.6 %last.1 = (bf16[8,32,128]{2,1,0:T(8,128)(2,1)}, bf16[8,32,128]{2,1,0:T(8,128)(2,1)}) custom-call(s32[1]{0:T(128)} %bitcast.me_ref, bf16[16,32,1536]{2,1,0:T(8,128)(2,1)} %get-tuple-element.94.joint, bf16[3,256,1792]{2,1,0:T(8,128)(2,1)} %get-tuple-element.95.dproj_a, bf16[3,256,1792]{2,1,0:T(8,128)(2,1)} %get-tuple-element.96.dproj_b, ...), custom_call_target="tpu_custom_call" | custom-call | flops 3000000000 | bytes 10485760 | tf_op jit(solution)/shard_map/last/pallas_call | solution.py:722
  280.4 0.6 add_convert_fusion
  281.2 1.6 collective-permute-start.15
  283.1 1.1 collective-permute-start.21
  284.3 0.4 collective-permute-done.26
  284.8 0.9 collective-permute-start.27
  285.7 29.5 %collective-permute-done.21 = bf16[4,192,128]{2,1,0:T(8,128)(2,1)S(1)} collective-permute-done((bf16[4,192,128]{2,1,0:T(8,128)(2,1)S(1)}, bf16[4,192,128]{2,1,0:T(8,128)(2,1)S(1)}, u32[]{:S(2)}, u32[]{:S(2)}) %collective-permute-start.21) | collective-permute-done | bytes 196640 | tf_op jit(solution)/shard_map/ppermute | solution.py:61
  315.3 11.7 %collective-permute-start.22 = (bf16[192,128]{1,0:T(8,128)(2,1)S(1)}, bf16[192,128]{1,0:T(8,128)(2,1)S(1)}, u32[]{:S(2)}, u32[]{:S(2)}) collective-permute-start(bf16[192,128]{1,0:T(8,128)(2,1)S(1)} %get-tuple-element.128), channel_id=1, source_target_pairs={{0,8},{2,10},{4,12},{6,14},{8,0},{10,2},{12,4},{14,6},{16,24},{18,... | collective-permute-start | bytes 147464 | tf_op jit(solution)/shard_map/ppermute | solution.py:61
  327.1 1.1 collective-permute-start.23
  328.6 2.0 collective-permute-start.16
  330.6 2.4 collective-permute-start.18
  333.2 9.3 %collective-permute-done.16 = bf16[1200,128]{1,0:T(8,128)(2,1)S(1)} collective-permute-done((bf16[1200,128]{1,0:T(8,128)(2,1)S(1)}, bf16[1200,128]{1,0:T(8,128)(2,1)S(1)}, u32[]{:S(2)}, u32[]{:S(2)}) %collective-permute-start.16) | collective-permute-done | bytes 307232 | tf_op jit(solution)/shard_map/ppermute | solution.py:61
  342.5 13.7 %collective-permute-done.17 = bf16[1200,128]{1,0:T(8,128)(2,1)S(1)} collective-permute-done((bf16[1200,128]{1,0:T(8,128)(2,1)S(1)}, bf16[1200,128]{1,0:T(8,128)(2,1)S(1)}, u32[]{:S(2)}, u32[]{:S(2)}) %collective-permute-start.17) | collective-permute-done | bytes 307232 | tf_op jit(solution)/shard_map/ppermute | solution.py:61
  356.2 1.3 collective-permute-start.30
  357.7 2.6 collective-permute-start.24
  360.3 4.8 %collective-permute-done.29 = bf16[224,128]{1,0:T(8,128)(2,1)S(1)} collective-permute-done((bf16[224,128]{1,0:T(8,128)(2,1)S(1)}, bf16[224,128]{1,0:T(8,128)(2,1)S(1)}, u32[]{:S(2)}, u32[]{:S(2)}) %collective-permute-start.29) | collective-permute-done | bytes 57376 | tf_op jit(solution)/shard_map/ppermute | solution.py:61
  365.1 1.5 collective-permute-start.19
  366.6 0.6 collective-permute-start.31
  367.3 1.6 collective-permute-start.25
  368.8 0.7 copy.61
  369.5 0.7 copy.62
  370.2 2.8 collective-permute-done.25.other_a
  373.1 0.6 copy-done.17
  373.7 2.2 step_first.1
  375.9 0.7 copy-done.11
  376.6 3.1 step_second.1
  379.8 1.4 copy.63
  381.2 1.4 copy.64
  382.5 1.4 copy.65
  (89 shorter events, 1.9 us)
Async XLA Ops:
  0.7 2.5 copy-start.4
  0.7 3.8 copy-start.5
  3.2 2.5 copy-start.18
  5.7 9.8 %copy-start.19 = (f32[1,4,32]{2,1,0:T(4,128)S(1)}, f32[1,4,32]{2,1,0:T(4,128)}, u32[]{:S(2)}) copy-start(f32[1,4,32]{2,1,0:T(4,128)} %param.35) | copy-start | bytes 1540
  12.6 23.5 %collective-permute-start = (f32[2,448,256]{2,1,0:T(8,128)}, f32[2,448,256]{2,1,0:T(8,128)S(1)}, u32[]{:S(2)}, u32[]{:S(2)}) collective-permute-start(f32[2,448,256]{2,1,0:T(8,128)} %get-tuple-element.73), channel_id=1, source_target_pairs={{0,1},{1,0},{2,3},{3,2},{4,5},{5,4},{6,7},{7,6},{8,9},{9,8},{10,11... | collective-permute-start | bytes 2752520 | tf_op jit(solution)/shard_map/ppermute | solution.py:61
  39.3 15.2 %collective-permute-start.1 = (bf16[1200,128]{1,0:T(8,128)(2,1)}, bf16[1200,128]{1,0:T(8,128)(2,1)S(1)}, u32[]{:S(2)}, u32[]{:S(2)}) collective-permute-start(bf16[1200,128]{1,0:T(8,128)(2,1)} %pack_second.1), channel_id=1, source_target_pairs={{0,8},{2,10},{4,12},{6,14},{8,0},{10,2},{12,4},{14,6},{16,24},{18,... | collective-permute-start | bytes 921608 | tf_op jit(solution)/shard_map/ppermute | solution.py:61
  41.1 29.0 %collective-permute-start.2 = (bf16[1200,128]{1,0:T(8,128)(2,1)}, bf16[1200,128]{1,0:T(8,128)(2,1)S(1)}, u32[]{:S(2)}, u32[]{:S(2)}) collective-permute-start(bf16[1200,128]{1,0:T(8,128)(2,1)} %pack_second.1), channel_id=1, source_target_pairs={{0,16},{2,18},{4,20},{6,22},{8,24},{10,26},{12,28},{14,30},{16,0},... | collective-permute-start | bytes 921608 | tf_op jit(solution)/shard_map/ppermute | solution.py:61
  43.7 26.5 %collective-permute-start.3 = (bf16[1200,128]{1,0:T(8,128)(2,1)}, bf16[1200,128]{1,0:T(8,128)(2,1)S(1)}, u32[]{:S(2)}, u32[]{:S(2)}) collective-permute-start(bf16[1200,128]{1,0:T(8,128)(2,1)} %pack_second.1), channel_id=1, source_target_pairs={{0,24},{2,26},{4,28},{6,30},{8,16},{10,18},{12,20},{14,22},{16,8},... | collective-permute-start | bytes 921608 | tf_op jit(solution)/shard_map/ppermute | solution.py:61
  45.3 32.6 %copy-start.6 = (bf16[416,128]{1,0:T(8,128)(2,1)S(1)}, bf16[416,128]{1,0:T(8,128)(2,1)}, u32[]{:S(2)}) copy-start(bf16[416,128]{1,0:T(8,128)(2,1)} %pack_first.1) | copy-start | bytes 319492
  45.3 27.7 %collective-permute-start.7 = (bf16[416,128]{1,0:T(8,128)(2,1)}, bf16[416,128]{1,0:T(8,128)(2,1)S(1)}, u32[]{:S(2)}, u32[]{:S(2)}) collective-permute-start(bf16[416,128]{1,0:T(8,128)(2,1)} %pack_first.1), channel_id=1, source_target_pairs={{0,8},{2,10},{4,12},{6,14},{8,0},{10,2},{12,4},{14,6},{16,24},{18,... | collective-permute-start | bytes 319496 | tf_op jit(solution)/shard_map/ppermute | solution.py:61
  46.2 31.7 %collective-permute-start.8 = (bf16[416,128]{1,0:T(8,128)(2,1)}, bf16[416,128]{1,0:T(8,128)(2,1)S(1)}, u32[]{:S(2)}, u32[]{:S(2)}) collective-permute-start(bf16[416,128]{1,0:T(8,128)(2,1)} %pack_first.1), channel_id=1, source_target_pairs={{0,16},{2,18},{4,20},{6,22},{8,24},{10,26},{12,28},{14,30},{16,0},... | collective-permute-start | bytes 319496 | tf_op jit(solution)/shard_map/ppermute | solution.py:61
  54.5 23.4 %collective-permute-start.9 = (bf16[416,128]{1,0:T(8,128)(2,1)}, bf16[416,128]{1,0:T(8,128)(2,1)S(1)}, u32[]{:S(2)}, u32[]{:S(2)}) collective-permute-start(bf16[416,128]{1,0:T(8,128)(2,1)} %pack_first.1), channel_id=1, source_target_pairs={{0,24},{2,26},{4,28},{6,30},{8,16},{10,18},{12,20},{14,22},{16,8},... | collective-permute-start | bytes 319496 | tf_op jit(solution)/shard_map/ppermute | solution.py:61
  70.2 32.3 %copy-start.3 = (f32[2,448,256]{2,1,0:T(8,128)S(1)}, f32[2,448,256]{2,1,0:T(8,128)}, u32[]{:S(2)}) copy-start(f32[2,448,256]{2,1,0:T(8,128)} %get-tuple-element.77) | copy-start | bytes 2752516
  71.4 40.0 %copy-start.1 = (bf16[4,1200,128]{2,1,0:T(8,128)(2,1)}, bf16[4,1200,128]{2,1,0:T(8,128)(2,1)S(1)}, u32[]{:S(2)}) copy-start(bf16[4,1200,128]{2,1,0:T(8,128)(2,1)S(1)} %pad_maximum_fusion.1.g0) | copy-start | bytes 3686404
  71.4 40.6 %collective-permute-start.4 = (bf16[4,1200,128]{2,1,0:T(8,128)(2,1)S(1)}, bf16[4,1200,128]{2,1,0:T(8,128)(2,1)}, u32[]{:S(2)}, u32[]{:S(2)}) collective-permute-start(bf16[4,1200,128]{2,1,0:T(8,128)(2,1)S(1)} %pad_maximum_fusion.1.g0), channel_id=1, source_target_pairs={{0,4},{2,6},{4,0},{6,2},{8,12},{10,14},{12,8},{14,10},{16,20},{18,... | collective-permute-start | bytes 3686408 | tf_op jit(solution)/shard_map/ppermute | solution.py:61
  78.0 25.9 %copy-start.7 = (bf16[4,416,128]{2,1,0:T(8,128)(2,1)}, bf16[4,416,128]{2,1,0:T(8,128)(2,1)S(1)}, u32[]{:S(2)}) copy-start(bf16[4,416,128]{2,1,0:T(8,128)(2,1)S(1)} %pad_maximum_fusion.4.g0) | copy-start | bytes 1277956
  78.0 22.6 %collective-permute-start.10 = (bf16[4,416,128]{2,1,0:T(8,128)(2,1)S(1)}, bf16[4,416,128]{2,1,0:T(8,128)(2,1)}, u32[]{:S(2)}, u32[]{:S(2)}) collective-permute-start(bf16[4,416,128]{2,1,0:T(8,128)(2,1)S(1)} %pad_maximum_fusion.4.g0), channel_id=1, source_target_pairs={{0,4},{2,6},{4,0},{6,2},{8,12},{10,14},{12,8},{14,10},{16,20},{18,... | collective-permute-start | bytes 1277960 | tf_op jit(solution)/shard_map/ppermute | solution.py:61
  79.6 21.1 %collective-permute-start.13 = (bf16[2,448,128]{2,1,0:T(8,128)(2,1)}, bf16[2,448,128]{2,1,0:T(8,128)(2,1)}, u32[]{:S(2)}, u32[]{:S(2)}) collective-permute-start(bf16[2,448,128]{2,1,0:T(8,128)(2,1)} %get-tuple-element.75), channel_id=1, source_target_pairs={{0,1},{1,0},{2,3},{3,2},{4,5},{5,4},{6,7},{7,6},{8,9},{9,8},{10,11... | collective-permute-start | bytes 688136 | tf_op jit(solution)/shard_map/ppermute | solution.py:61
  81.1 22.8 %collective-permute-start.11 = (bf16[4,416,128]{2,1,0:T(8,128)(2,1)S(1)}, bf16[4,416,128]{2,1,0:T(8,128)(2,1)}, u32[]{:S(2)}, u32[]{:S(2)}) collective-permute-start(bf16[4,416,128]{2,1,0:T(8,128)(2,1)S(1)} %pad_maximum_fusion.4.g0), channel_id=1, source_target_pairs={{0,2},{2,0},{4,6},{6,4},{8,10},{10,8},{12,14},{14,12},{16,18},{18,... | collective-permute-start | bytes 1277960 | tf_op jit(solution)/shard_map/ppermute | solution.py:61
  100.6 3.2 collective-permute-start.12
  111.4 46.6 %collective-permute-start.5 = (bf16[4,1200,128]{2,1,0:T(8,128)(2,1)S(1)}, bf16[4,1200,128]{2,1,0:T(8,128)(2,1)S(1)}, u32[]{:S(2)}, u32[]{:S(2)}) collective-permute-start(bf16[4,1200,128]{2,1,0:T(8,128)(2,1)S(1)} %pad_maximum_fusion.1.g0), channel_id=1, source_target_pairs={{0,2},{2,0},{4,6},{6,4},{8,10},{10,8},{12,14},{14,12},{16,18},{18,... | collective-permute-start | bytes 3686408 | tf_op jit(solution)/shard_map/ppermute | solution.py:61
  112.0 46.1 %collective-permute-start.6 = (bf16[4,1200,128]{2,1,0:T(8,128)(2,1)}, bf16[4,1200,128]{2,1,0:T(8,128)(2,1)}, u32[]{:S(2)}, u32[]{:S(2)}) collective-permute-start(bf16[4,1200,128]{2,1,0:T(8,128)(2,1)} %collective-permute-done.4.g1), channel_id=1, source_target_pairs={{0,2},{2,0},{4,6},{6,4},{8,10},{10,8},{12,14},{14,12},{16,18},{18,... | collective-permute-start | bytes 3686408 | tf_op jit(solution)/shard_map/ppermute | solution.py:61
  158.1 1.0 copy-start.22
  218.7 61.6 %collective-permute-start.14 = (bf16[8,1200,128]{2,1,0:T(8,128)(2,1)}, bf16[8,1200,128]{2,1,0:T(8,128)(2,1)S(1)}, u32[]{:S(2)}, u32[]{:S(2)}) collective-permute-start(bf16[8,1200,128]{2,1,0:T(8,128)(2,1)} %get-tuple-element.82), channel_id=1, source_target_pairs={{0,2},{2,0},{4,6},{6,4},{8,10},{10,8},{12,14},{14,12},{16,18},{18,... | collective-permute-start | bytes 7372808 | tf_op jit(solution)/shard_map/ppermute | solution.py:61
  244.8 38.2 %collective-permute-start.20 = (bf16[8,192,128]{2,1,0:T(8,128)(2,1)}, bf16[8,192,128]{2,1,0:T(8,128)(2,1)S(1)}, u32[]{:S(2)}, u32[]{:S(2)}) collective-permute-start(bf16[8,192,128]{2,1,0:T(8,128)(2,1)} %get-tuple-element.90), channel_id=1, source_target_pairs={{0,2},{2,0},{4,6},{6,4},{8,10},{10,8},{12,14},{14,12},{16,18},{18,... | collective-permute-start | bytes 1179656 | tf_op jit(solution)/shard_map/ppermute | solution.py:61
  270.7 9.7 %copy-start = (bf16[8,1200,128]{2,1,0:T(8,128)(2,1)S(1)}, bf16[8,1200,128]{2,1,0:T(8,128)(2,1)}, u32[]{:S(2)}) copy-start(bf16[8,1200,128]{2,1,0:T(8,128)(2,1)} %get-tuple-element.81) | copy-start | bytes 7372804
  281.0 1.7 copy-start.8
  281.0 1.7 copy-start.14
  281.0 2.0 copy-start.10
  281.1 3.5 copy-start.9
  281.1 3.5 copy-start.15
  281.2 47.0 %collective-permute-start.15 = (bf16[4,1200,128]{2,1,0:T(8,128)(2,1)S(1)}, bf16[4,1200,128]{2,1,0:T(8,128)(2,1)S(1)}, u32[]{:S(2)}, u32[]{:S(2)}) collective-permute-start(bf16[4,1200,128]{2,1,0:T(8,128)(2,1)S(1)} %slice.78), channel_id=1, source_target_pairs={{0,4},{2,6},{4,0},{6,2},{8,12},{10,14},{12,8},{14,10},{16,20},{18,... | collective-permute-start | bytes 3686408 | tf_op jit(solution)/shard_map/ppermute | solution.py:61
  282.8 1.9 collective-permute-start.26
  283.1 32.1 %collective-permute-start.21 = (bf16[4,192,128]{2,1,0:T(8,128)(2,1)S(1)}, bf16[4,192,128]{2,1,0:T(8,128)(2,1)S(1)}, u32[]{:S(2)}, u32[]{:S(2)}) collective-permute-start(bf16[4,192,128]{2,1,0:T(8,128)(2,1)S(1)} %slice.84), channel_id=1, source_target_pairs={{0,4},{2,6},{4,0},{6,2},{8,12},{10,14},{12,8},{14,10},{16,20},{18,... | collective-permute-start | bytes 589832 | tf_op jit(solution)/shard_map/ppermute | solution.py:61
  284.8 45.8 %collective-permute-start.27 = (bf16[4,224,128]{2,1,0:T(8,128)(2,1)S(1)}, bf16[4,224,128]{2,1,0:T(8,128)(2,1)S(1)}, u32[]{:S(2)}, u32[]{:S(2)}) collective-permute-start(bf16[4,224,128]{2,1,0:T(8,128)(2,1)S(1)} %slice.90), channel_id=1, source_target_pairs={{0,4},{2,6},{4,0},{6,2},{8,12},{10,14},{12,8},{14,10},{16,20},{18,... | collective-permute-start | bytes 688136 | tf_op jit(solution)/shard_map/ppermute | solution.py:61
  315.3 51.9 %collective-permute-start.22 = (bf16[192,128]{1,0:T(8,128)(2,1)S(1)}, bf16[192,128]{1,0:T(8,128)(2,1)S(1)}, u32[]{:S(2)}, u32[]{:S(2)}) collective-permute-start(bf16[192,128]{1,0:T(8,128)(2,1)S(1)} %get-tuple-element.128), channel_id=1, source_target_pairs={{0,8},{2,10},{4,12},{6,14},{8,0},{10,2},{12,4},{14,6},{16,24},{18,... | collective-permute-start | bytes 147464 | tf_op jit(solution)/shard_map/ppermute | solution.py:61
  327.1 40.1 %collective-permute-start.23 = (bf16[192,128]{1,0:T(8,128)(2,1)S(1)}, bf16[192,128]{1,0:T(8,128)(2,1)S(1)}, u32[]{:S(2)}, u32[]{:S(2)}) collective-permute-start(bf16[192,128]{1,0:T(8,128)(2,1)S(1)} %get-tuple-element.130), channel_id=1, source_target_pairs={{0,16},{2,18},{4,20},{6,22},{8,24},{10,26},{12,28},{14,30},{16,0},... | collective-permute-start | bytes 147464 | tf_op jit(solution)/shard_map/ppermute | solution.py:61
  328.6 40.2 %copy-start.20 = (f32[1,4,32]{2,1,0:T(4,128)S(1)}, f32[1,4,32]{2,1,0:T(4,128)}, u32[]{:S(2)}) copy-start(f32[1,4,32]{2,1,0:T(4,128)} %param.42) | copy-start | bytes 1540
  328.6 40.9 %copy-start.21 = (f32[1,4,32]{2,1,0:T(4,128)S(1)}, f32[1,4,32]{2,1,0:T(4,128)}, u32[]{:S(2)}) copy-start(f32[1,4,32]{2,1,0:T(4,128)} %param.49) | copy-start | bytes 1540
  328.6 13.8 %collective-permute-start.16 = (bf16[1200,128]{1,0:T(8,128)(2,1)S(1)}, bf16[1200,128]{1,0:T(8,128)(2,1)S(1)}, u32[]{:S(2)}, u32[]{:S(2)}) collective-permute-start(bf16[1200,128]{1,0:T(8,128)(2,1)S(1)} %get-tuple-element.122), channel_id=1, source_target_pairs={{0,8},{2,10},{4,12},{6,14},{8,0},{10,2},{12,4},{14,6},{16,24},{18,... | collective-permute-start | bytes 921608 | tf_op jit(solution)/shard_map/ppermute | solution.py:61
  330.6 25.5 %collective-permute-start.17 = (bf16[1200,128]{1,0:T(8,128)(2,1)S(1)}, bf16[1200,128]{1,0:T(8,128)(2,1)S(1)}, u32[]{:S(2)}, u32[]{:S(2)}) collective-permute-start(bf16[1200,128]{1,0:T(8,128)(2,1)S(1)} %get-tuple-element.124), channel_id=1, source_target_pairs={{0,16},{2,18},{4,20},{6,22},{8,24},{10,26},{12,28},{14,30},{16,0},... | collective-permute-start | bytes 921608 | tf_op jit(solution)/shard_map/ppermute | solution.py:61
  330.6 25.5 %collective-permute-start.18 = (bf16[1200,128]{1,0:T(8,128)(2,1)S(1)}, bf16[1200,128]{1,0:T(8,128)(2,1)S(1)}, u32[]{:S(2)}, u32[]{:S(2)}) collective-permute-start(bf16[1200,128]{1,0:T(8,128)(2,1)S(1)} %get-tuple-element.123), channel_id=1, source_target_pairs={{0,24},{2,26},{4,28},{6,30},{8,16},{10,18},{12,20},{14,22},{16,8},... | collective-permute-start | bytes 921608 | tf_op jit(solution)/shard_map/ppermute | solution.py:61
  342.5 15.2 %collective-permute-start.28 = (bf16[224,128]{1,0:T(8,128)(2,1)S(1)}, bf16[224,128]{1,0:T(8,128)(2,1)S(1)}, u32[]{:S(2)}, u32[]{:S(2)}) collective-permute-start(bf16[224,128]{1,0:T(8,128)(2,1)S(1)} %get-tuple-element.125), channel_id=1, source_target_pairs={{0,8},{2,10},{4,12},{6,14},{8,0},{10,2},{12,4},{14,6},{16,24},{18,... | collective-permute-start | bytes 172040 | tf_op jit(solution)/shard_map/ppermute | solution.py:61
  356.2 8.9 %collective-permute-start.29 = (bf16[224,128]{1,0:T(8,128)(2,1)S(1)}, bf16[224,128]{1,0:T(8,128)(2,1)S(1)}, u32[]{:S(2)}, u32[]{:S(2)}) collective-permute-start(bf16[224,128]{1,0:T(8,128)(2,1)S(1)} %get-tuple-element.127), channel_id=1, source_target_pairs={{0,16},{2,18},{4,20},{6,22},{8,24},{10,26},{12,28},{14,30},{16,0},... | collective-permute-start | bytes 172040 | tf_op jit(solution)/shard_map/ppermute | solution.py:61
  356.2 10.4 %collective-permute-start.30 = (bf16[224,128]{1,0:T(8,128)(2,1)S(1)}, bf16[224,128]{1,0:T(8,128)(2,1)S(1)}, u32[]{:S(2)}, u32[]{:S(2)}) collective-permute-start(bf16[224,128]{1,0:T(8,128)(2,1)S(1)} %get-tuple-element.126), channel_id=1, source_target_pairs={{0,24},{2,26},{4,28},{6,30},{8,16},{10,18},{12,20},{14,22},{16,8},... | collective-permute-start | bytes 172040 | tf_op jit(solution)/shard_map/ppermute | solution.py:61
  357.7 18.2 %copy-start.2 = (bf16[1200,128]{1,0:T(8,128)(2,1)}, bf16[1200,128]{1,0:T(8,128)(2,1)S(1)}, u32[]{:S(2)}) copy-start(bf16[1200,128]{1,0:T(8,128)(2,1)S(1)} %fusion.2.mine) | copy-start | bytes 921604
  357.7 9.5 %collective-permute-start.24 = (bf16[192,128]{1,0:T(8,128)(2,1)S(1)}, bf16[192,128]{1,0:T(8,128)(2,1)S(1)}, u32[]{:S(2)}, u32[]{:S(2)}) collective-permute-start(bf16[192,128]{1,0:T(8,128)(2,1)S(1)} %get-tuple-element.129), channel_id=1, source_target_pairs={{0,24},{2,26},{4,28},{6,30},{8,16},{10,18},{12,20},{14,22},{16,8},... | collective-permute-start | bytes 147464 | tf_op jit(solution)/shard_map/ppermute | solution.py:61
  365.1 10.9 %collective-permute-start.19 = (bf16[1200,128]{1,0:T(8,128)(2,1)S(1)}, bf16[1200,128]{1,0:T(8,128)(2,1)S(1)}, u32[]{:S(2)}, u32[]{:S(2)}) collective-permute-start(bf16[1200,128]{1,0:T(8,128)(2,1)S(1)} %fusion.2.mine), channel_id=1, source_target_pairs={{0,1},{1,0},{2,3},{3,2},{4,5},{5,4},{6,7},{7,6},{8,9},{9,8},{10,11... | collective-permute-start | bytes 921608 | tf_op jit(solution)/shard_map/ppermute | solution.py:61
  366.6 6.5 %copy-start.12 = (bf16[224,128]{1,0:T(8,128)(2,1)}, bf16[224,128]{1,0:T(8,128)(2,1)S(1)}, u32[]{:S(2)}) copy-start(bf16[224,128]{1,0:T(8,128)(2,1)S(1)} %fusion.5.mine_b) | copy-start | bytes 172036
  366.6 6.4 %collective-permute-start.31 = (bf16[224,128]{1,0:T(8,128)(2,1)S(1)}, bf16[224,128]{1,0:T(8,128)(2,1)S(1)}, u32[]{:S(2)}, u32[]{:S(2)}) collective-permute-start(bf16[224,128]{1,0:T(8,128)(2,1)S(1)} %fusion.5.mine_b), channel_id=1, source_target_pairs={{0,1},{1,0},{2,3},{3,2},{4,5},{5,4},{6,7},{7,6},{8,9},{9,8},{10,11... | collective-permute-start | bytes 172040 | tf_op jit(solution)/shard_map/ppermute | solution.py:61
  367.3 5.8 %copy-start.13 = (bf16[192,128]{1,0:T(8,128)(2,1)}, bf16[192,128]{1,0:T(8,128)(2,1)S(1)}, u32[]{:S(2)}) copy-start(bf16[192,128]{1,0:T(8,128)(2,1)S(1)} %fusion.8.mine_a) | copy-start | bytes 147460
  367.3 5.8 %collective-permute-start.25 = (bf16[192,128]{1,0:T(8,128)(2,1)S(1)}, bf16[192,128]{1,0:T(8,128)(2,1)S(1)}, u32[]{:S(2)}, u32[]{:S(2)}) collective-permute-start(bf16[192,128]{1,0:T(8,128)(2,1)S(1)} %fusion.8.mine_a), channel_id=1, source_target_pairs={{0,1},{1,0},{2,3},{3,2},{4,5},{5,4},{6,7},{7,6},{8,9},{9,8},{10,11... | collective-permute-start | bytes 147464 | tf_op jit(solution)/shard_map/ppermute | solution.py:61
  373.1 0.6 copy-start.17
  373.1 0.6 copy-start.16
  375.9 0.7 copy-start.11
